TPU v7x, 256 devices: a whole 4x4x8 slice. The times are simulated.
256 devices in a mesh: dp: 128 (over y, z_lo, x, core), tensor: 2 (over z_hi).
Axes of the slice: x: 4, y: 4, z: 8 (z_hi: 2, z_lo: 4; z = z_hi * 4 + z_lo), core: 2. Of those that a mesh axis runs over, the one named last changes fastest.
Arguments:
- activations: bfloat16 [65536, 5120], P('dp'), may hold values from -60 to 60
- kv_cotangents: bfloat16 [65536, 8, 256], P('dp', 'tensor'), may hold values from -4 to 4
Outputs:
- combined_grad: float32 [5120, 8, 256], P('dp', 'tensor')
All inputs are finite; a program needn't handle non-finite values.
Results may differ from a plain program's by a relative error of at most 0.0011.
Values may be sent and summed in bfloat16 or wider, within the bound.
A program may use at most 128 MiB of HBM per device.

v0:
```python
import jax
import jax.numpy as jnp
from jax import lax
from jax.sharding import PartitionSpec as P

epsilon = 1e-06


def swapped(block, axis, apart):
    count = lax.axis_size(axis)
    route = []
    for low in range(count):
        high = low | 1 << apart
        if high != low and high < count:
            route += [(low, high), (high, low)]
    return lax.ppermute(block, axis, route)


def contract_tokens(left_rows, right_rows):
    return lax.dot_general(
        left_rows, right_rows, (((0,), (0,)), ((), ())), preferred_element_type=jnp.float32
    )


def group_sums(partials, level_index, position, replicas):
    groups = replicas >> level_index + 1
    group_mask = (jnp.arange(groups, dtype=jnp.int32) == position >> level_index + 1).astype(
        jnp.float32
    )
    slot_table = lax.psum(partials[:, None] * group_mask[None, :], ("dp", "tensor"))
    return jnp.sum(slot_table * group_mask[None, :], axis=1)


def merge_level(kept_part, received, level_index, position, replicas):
    lower_side = (position >> level_index) % 2 == 0
    own_sq = jnp.sum(kept_part * kept_part)
    other_sq = jnp.sum(received * received)
    cross_sum = jnp.sum(kept_part * received)
    partials = jnp.stack(
        [
            cross_sum,
            jnp.where(lower_side, own_sq, other_sq),
            jnp.where(lower_side, other_sq, own_sq),
        ]
    )
    totals = group_sums(partials, level_index, position, replicas)
    lower_coef = 1.0 - totals[0] / (2.0 * totals[1] + epsilon)
    upper_coef = 1.0 - totals[0] / (2.0 * totals[2] + epsilon)
    own_coef = jnp.where(lower_side, lower_coef, upper_coef)
    other_coef = jnp.where(lower_side, upper_coef, lower_coef)
    return own_coef * kept_part + other_coef * received


def body(activations, kv_cotangents):
    tok_rows, feat_count = activations.shape
    columns = kv_cotangents.shape[1] * kv_cotangents.shape[2]
    kv_deltas = kv_cotangents.reshape(tok_rows, columns)
    replicas = lax.axis_size("dp")
    levels = replicas.bit_length() - 1
    seg_rows = feat_count // replicas
    position = lax.axis_index("dp")
    first_bit = position % 2
    gradient = contract_tokens(activations, kv_deltas).astype(jnp.bfloat16)
    halves_view = gradient.reshape(replicas // 2, 2, seg_rows, columns)
    kept_part = lax.dynamic_index_in_dim(halves_view, first_bit, 1, keepdims=False)
    outgoing = lax.dynamic_index_in_dim(halves_view, 1 - first_bit, 1, keepdims=False)
    received = swapped(outgoing, "dp", 0)
    kept_part = kept_part.astype(jnp.float32)
    received = received.astype(jnp.float32)
    segment_part = merge_level(kept_part, received, 0, position, replicas)
    for level_index in range(1, levels):
        level_bit = (position >> level_index) % 2
        halves_view = segment_part.reshape(segment_part.shape[0] // 2, 2, seg_rows, columns)
        kept_part = lax.dynamic_index_in_dim(halves_view, level_bit, 1, keepdims=False)
        outgoing = lax.dynamic_index_in_dim(halves_view, 1 - level_bit, 1, keepdims=False)
        received = swapped(outgoing, "dp", level_index)
        segment_part = merge_level(kept_part, received, level_index, position, replicas)
    return segment_part.reshape(seg_rows, kv_cotangents.shape[1], kv_cotangents.shape[2])


def solution(mesh):
    return jax.shard_map(
        body,
        mesh=mesh,
        in_specs=(P("dp", None), P("dp", "tensor", None)),
        out_specs=P("dp", "tensor", None),
        check_vma=False,
    )
```

profile of v0, /device:TPU:1, one launch (start us, length us, event | category | flops | bytes accessed | tf_op | source)
XLA Modules:
  0.0 898.5 jit_solution(10929016668822143682)
XLA Ops:
  0.0 1.4 copy.11
  1.5 8.4 convolution_convert_fusion
  9.9 3.6 dynamic-slice_bitcast_fusion.1
  13.4 2.0 copy-done.2
  15.4 3.2 collective-permute-start
  18.6 8.6 collective-permute-done
  27.2 7.4 fusion.2
  38.0 78.8 %psum.49 = f32[3,64]{1,0:T(4,128)S(1)} all-reduce(f32[3,64]{1,0:T(4,128)S(1)} %broadcast_multiply_fusion.4), channel_id=1, replica_groups=mesh['dp'=128,'tensor'=2] {'dp','tensor'}, use_global_device_ids=true, to_apply=%region_3.4 | all-reduce | flops 192 | bytes 1536 | tf_op jit(solution)/shard_map/psum | solution.py:30
  120.2 6.6 fusion.1
  126.8 3.0 dynamic-slice_bitcast_fusion
  129.8 2.6 copy-done
  132.4 113.9 %collective-permute-done.1 = f32[32,40,1024]{2,1,0:T(8,128)} collective-permute-done((f32[32,40,1024]{2,1,0:T(8,128)}, f32[32,40,1024]{2,1,0:T(8,128)}, u32[]{:S(2)}, u32[]{:S(2)}) %collective-permute-start.1) | collective-permute-done | bytes 5242912 | tf_op jit(solution)/shard_map/ppermute | solution.py:16
  246.3 6.1 fusion.4
  255.8 72.7 %psum.50 = f32[3,32]{1,0:T(4,128)S(1)} all-reduce(f32[3,32]{1,0:T(4,128)S(1)} %broadcast_multiply_fusion.3), channel_id=1, replica_groups=mesh['dp'=128,'tensor'=2] {'dp','tensor'}, use_global_device_ids=true, to_apply=%region_8.9 | all-reduce | flops 96 | bytes 768 | tf_op jit(solution)/shard_map/psum | solution.py:30
  331.8 5.3 fusion.6
  337.1 2.3 copy-done.1
  339.4 1.7 dynamic-slice_bitcast_fusion.2
  342.3 58.3 %collective-permute-done.2 = f32[16,40,1024]{2,1,0:T(8,128)S(1)} collective-permute-done((f32[16,40,1024]{2,1,0:T(8,128)}, f32[16,40,1024]{2,1,0:T(8,128)S(1)}, u32[]{:S(2)}, u32[]{:S(2)}) %collective-permute-start.2) | collective-permute-done | bytes 2621472 | tf_op jit(solution)/shard_map/ppermute | solution.py:16
  400.5 4.0 fusion.7
  407.9 75.1 %psum.51 = f32[3,16]{1,0:T(4,128)S(1)} all-reduce(f32[3,16]{1,0:T(4,128)S(1)} %broadcast_multiply_fusion.2), channel_id=1, replica_groups=mesh['dp'=128,'tensor'=2] {'dp','tensor'}, use_global_device_ids=true, to_apply=%region_13.14 | all-reduce | flops 48 | bytes 384 | tf_op jit(solution)/shard_map/psum | solution.py:30
  486.3 3.1 fusion.9
  491.7 28.9 %collective-permute-done.3 = f32[8,40,1024]{2,1,0:T(8,128)} collective-permute-done((f32[8,40,1024]{2,1,0:T(8,128)}, f32[8,40,1024]{2,1,0:T(8,128)}, u32[]{:S(2)}, u32[]{:S(2)}) %collective-permute-start.3) | collective-permute-done | bytes 1310752 | tf_op jit(solution)/shard_map/ppermute | solution.py:16
  520.6 2.3 fusion.10
  526.2 73.4 %psum.52 = f32[3,8]{1,0:T(4,128)S(1)} all-reduce(f32[3,8]{1,0:T(4,128)S(1)} %broadcast_multiply_fusion.1), channel_id=1, replica_groups=mesh['dp'=128,'tensor'=2] {'dp','tensor'}, use_global_device_ids=true, to_apply=%region_18.19 | all-reduce | flops 24 | bytes 192 | tf_op jit(solution)/shard_map/psum | solution.py:30
  602.9 1.6 fusion.12
  605.9 30.3 %collective-permute-done.4 = f32[4,40,1024]{2,1,0:T(8,128)S(1)} collective-permute-done((f32[4,40,1024]{2,1,0:T(8,128)S(1)}, f32[4,40,1024]{2,1,0:T(8,128)S(1)}, u32[]{:S(2)}, u32[]{:S(2)}) %collective-permute-start.4) | collective-permute-done | bytes 655392 | tf_op jit(solution)/shard_map/ppermute | solution.py:16
  636.2 1.9 fusion.13
  641.4 73.8 %psum.53 = f32[3,4]{1,0:T(4,128)S(1)} all-reduce(f32[3,4]{1,0:T(4,128)S(1)} %broadcast_multiply_fusion), channel_id=1, replica_groups=mesh['dp'=128,'tensor'=2] {'dp','tensor'}, use_global_device_ids=true, to_apply=%region_23.24 | all-reduce | flops 12 | bytes 96 | tf_op jit(solution)/shard_map/psum | solution.py:30
  720.6 7.7 collective-permute-done.5
  732.4 74.4 %psum.54 = f32[3,2]{0,1:T(2,128)S(1)} all-reduce(f32[3,2]{0,1:T(2,128)S(1)} %broadcast_multiply_fusion.5), channel_id=1, replica_groups=mesh['dp'=128,'tensor'=2] {'dp','tensor'}, use_global_device_ids=true, to_apply=%region_28.29 | all-reduce | flops 6 | bytes 48 | tf_op jit(solution)/shard_map/psum | solution.py:30
  811.4 5.5 collective-permute-done.6
  820.8 73.7 %psum.55 = f32[3,1]{0,1:T(1,128)S(1)} all-reduce(f32[3,1]{0,1:T(1,128)S(1)} %maximum_multiply_fusion), channel_id=1, replica_groups=mesh['dp'=128,'tensor'=2] {'dp','tensor'}, use_global_device_ids=true, to_apply=%region_33.34 | all-reduce | flops 3 | bytes 24 | tf_op jit(solution)/shard_map/psum | solution.py:30
  (56 shorter events, 21.2 us)
Async XLA Ops:
  9.8 5.5 copy-start.2
  15.4 11.9 %collective-permute-start = (bf16[64,40,1024]{2,1,0:T(8,128)(2,1)}, bf16[64,40,1024]{2,1,0:T(8,128)(2,1)}, u32[]{:S(2)}, u32[]{:S(2)}) collective-permute-start(bf16[64,40,1024]{2,1,0:T(8,128)(2,1)} %dynamic-slice_bitcast_fusion.1), channel_id=1, source_target_pairs={{0,2},{2,0},{4,6},{6,4},{8,10},{10,8},{12,14},{14,12},{16,18},{18,... | collective-permute-start | bytes 15728648 | tf_op jit(solution)/shard_map/ppermute | solution.py:16
  126.8 5.6 copy-start
  132.4 113.9 %collective-permute-start.1 = (f32[32,40,1024]{2,1,0:T(8,128)}, f32[32,40,1024]{2,1,0:T(8,128)}, u32[]{:S(2)}, u32[]{:S(2)}) collective-permute-start(f32[32,40,1024]{2,1,0:T(8,128)} %dynamic-slice_bitcast_fusion), channel_id=1, source_target_pairs={{0,4},{4,0},{2,6},{6,2},{8,12},{12,8},{10,14},{14,10},{16,20},{20,... | collective-permute-start | bytes 15728648 | tf_op jit(solution)/shard_map/ppermute | solution.py:16
  337.1 2.3 copy-start.1
  341.1 59.4 %collective-permute-start.2 = (f32[16,40,1024]{2,1,0:T(8,128)}, f32[16,40,1024]{2,1,0:T(8,128)S(1)}, u32[]{:S(2)}, u32[]{:S(2)}) collective-permute-start(f32[16,40,1024]{2,1,0:T(8,128)} %dynamic-slice_bitcast_fusion.2), channel_id=1, source_target_pairs={{0,8},{8,0},{2,10},{10,2},{4,12},{12,4},{6,14},{14,6},{16,24},{24,... | collective-permute-start | bytes 7864328 | tf_op jit(solution)/shard_map/ppermute | solution.py:16
  400.5 85.8 %copy-start.3 = (f32[16,40,1024]{2,1,0:T(8,128)}, f32[16,40,1024]{2,1,0:T(8,128)S(1)}, u32[]{:S(2)}) copy-start(f32[16,40,1024]{2,1,0:T(8,128)S(1)} %collective-permute-done.2) | copy-start | bytes 7864324
  490.6 30.0 %collective-permute-start.3 = (f32[8,40,1024]{2,1,0:T(8,128)}, f32[8,40,1024]{2,1,0:T(8,128)}, u32[]{:S(2)}, u32[]{:S(2)}) collective-permute-start(f32[8,40,1024]{2,1,0:T(8,128)} %dynamic-slice_bitcast_fusion.3), channel_id=1, source_target_pairs={{0,16},{16,0},{2,18},{18,2},{4,20},{20,4},{6,22},{22,6},{8,24},{24... | collective-permute-start | bytes 3932168 | tf_op jit(solution)/shard_map/ppermute | solution.py:16
  604.4 1.1 copy-start.4
  605.5 30.6 %collective-permute-start.4 = (f32[4,40,1024]{2,1,0:T(8,128)S(1)}, f32[4,40,1024]{2,1,0:T(8,128)S(1)}, u32[]{:S(2)}, u32[]{:S(2)}) collective-permute-start(f32[4,40,1024]{2,1,0:T(8,128)S(1)} %dynamic-slice_bitcast_fusion.4), channel_id=1, source_target_pairs={{0,32},{32,0},{2,34},{34,2},{4,36},{36,4},{6,38},{38,6},{8,40},{40... | collective-permute-start | bytes 1966088 | tf_op jit(solution)/shard_map/ppermute | solution.py:16
  719.7 8.7 collective-permute-start.5
  810.2 6.7 collective-permute-start.6
where the time goes:
time: 900 us; the launch traced here: 898 us
  blocking collectives  522 us (58%)
  waiting for transfers between devices  253 us (28%)
  other arithmetic  47.4 us (5%)
  between operations  35.6 us (4%)
  local copies, waits for them, and re-layouts  24.2 us (3%)
    psum x7, blocking collectives, group_sums(): lax.psum(partials[:, None] * group_mask[None, :], ('dp', 'tensor'))  522 us
    ppermute x7, waiting for transfers between devices, swapped(): return lax.ppermute(block, axis, route)  253 us
    reduce_sum x7, other arithmetic, merge_level(): cross_sum = jnp.sum(kept_part * received)  23.3 us
  transfers between devices with their start and end apart: 7, of which 7 were waited for; matrix products, arithmetic and copies ran while one was open for 0% of the time, Pallas kernels for 0%

commit v1 on v0

v1 whole, which is shorter than its diff:
```python
import functools

import jax
import jax.numpy as jnp
from jax import lax
from jax.experimental import pallas as pl
from jax.experimental.pallas import tpu as pltpu
from jax.sharding import PartitionSpec as P

MESH = pl.DeviceIdType.MESH
F32 = jnp.float32
BF16 = jnp.bfloat16
EPS = 1e-6
POWER = 9
TOP = 2.0**13
HALF = 2560
TILE = 640
BLOCK = 80
COLS = 1024


def coords(dp):
    return dp // 32, (dp // 8) % 4, (dp // 2) % 4, dp % 2


def rank(y, z, x, c):
    return ((y * 4 + z) * 4 + x) * 2 + c


def encode(v):
    v2 = v * v
    v4 = v2 * v2
    return (v4 * v4 * v).astype(BF16)


def decode(code):
    y = code.astype(F32)
    size = jnp.exp2(jnp.log2(jnp.abs(y)) * (1.0 / POWER))
    return jnp.where(y < 0, -size, size)


def iotas(rows):
    shape = (rows, 128)
    return (
        lax.broadcasted_iota(jnp.int32, shape, 0),
        lax.broadcasted_iota(jnp.int32, shape, 1),
    )


def partner_rows(gram, bit):
    rows = gram.shape[0]
    if bit == 8:
        return jnp.concatenate([gram[8:16], gram[0:8]], axis=0)
    parts = []
    for first in range(0, rows, 8):
        part = gram[first : first + 8]
        row = lax.broadcasted_iota(jnp.int32, part.shape, 0)
        parts.append(
            jnp.where((row & bit) == 0, pltpu.roll(part, 8 - bit, 0), pltpu.roll(part, bit, 0))
        )
    return parts[0] if len(parts) == 1 else jnp.concatenate(parts, axis=0)


def partner_lanes(gram, bit):
    lane = lax.broadcasted_iota(jnp.int32, gram.shape, 1)
    return jnp.where((lane & bit) == 0, pltpu.roll(gram, 128 - bit, 1), pltpu.roll(gram, bit, 1))


def solve(gram, count):
    rows = gram.shape[0]
    row, lane = iotas(rows)
    on_diag = row == lane
    first_diag = jnp.sum(jnp.where(on_diag, gram, 0.0), axis=1, keepdims=True)
    weight = jnp.ones((rows, 1), F32)
    bit = 1
    while bit < count:
        paired = (row ^ bit) == lane
        kept = jnp.where(on_diag, gram, 0.0)
        crossed = jnp.where(paired, gram, 0.0)
        col = 1.0 - jnp.sum(crossed, axis=1, keepdims=True) / (
            2.0 * jnp.sum(kept, axis=1, keepdims=True) + EPS
        )
        across = 1.0 - jnp.sum(crossed, axis=0, keepdims=True) / (
            2.0 * jnp.sum(kept, axis=0, keepdims=True) + EPS
        )
        weight = weight * col
        gram = gram * col * across
        if bit * 2 < count:
            gram = gram + partner_rows(gram, bit)
            gram = gram + partner_lanes(gram, bit)
        bit *= 2
    bound = float(count) * jnp.sum(weight * weight * first_diag, axis=0, keepdims=True) + 1e-36
    return weight, bound


def scalars(column, count):
    row = lax.broadcasted_iota(jnp.int32, column.shape, 0)
    return [jnp.sum(jnp.where(row == i, column, 0.0)) for i in range(count)]


def kernel(
    a_hbm, k_hbm, o_ref,
    a_own, a_oth, k_own, k_oth, a_t, grads, enc_x, recv_x, dec_x, enc_y, recv_y, recv_z, dec_z,
    rows_s, msg, slots0, slots1, slots2, slots3,
    load_sem, tok_send, tok_recv, x_send, x_recv, y_send, y_recv, z_send, z_recv, r_send, r_recv,
):
    me = lax.axis_index("dp")
    t = lax.axis_index("tensor")
    y, z, x, c = coords(me)
    row8, lane8 = iotas(8)

    def group16(k):
        return rank(y, z, (x + k // 4) % 4, (c + (k // 2) % 2) % 2), (t + k % 2) % 2

    def plane16(k):
        return rank((y + k // 4) % 4, (z + k % 4) % 4, x, c), t

    barrier = pltpu.get_barrier_semaphore()

    def greet_group(k, _):
        pl.semaphore_signal(barrier, inc=1, device_id=group16(k), device_id_type=MESH)
        return _

    def greet_plane(k, _):
        pl.semaphore_signal(barrier, inc=1, device_id=plane16(k), device_id_type=MESH)
        return _

    def greet_other(k, _):
        pl.semaphore_signal(
            barrier, inc=1, device_id=(rank((y + k) % 4, z, x, 1 - c), t), device_id_type=MESH
        )
        return _

    def a_cols(core, i):
        return pl.ds(pl.multiple_of(core * HALF + i * TILE, 128), TILE)

    load_k = pltpu.make_async_copy(k_hbm, k_own, load_sem.at[4])
    load_k.start()
    load_a = [
        pltpu.make_async_copy(a_hbm.at[:, a_cols(c, i)], a_own.at[i], load_sem.at[i])
        for i in range(4)
    ]
    for copy in load_a:
        copy.start()
    lax.fori_loop(1, 16, greet_group, 0)
    lax.fori_loop(1, 16, greet_plane, 0)
    lax.fori_loop(1, 4, greet_other, 0)

    def gradient_tile(a_ref, k_ref, which, i):
        a_t[...] = a_ref[i].T

        def columns(n, _):
            at = pl.ds(pl.multiple_of(n * 256, 256), 256)
            tile = jnp.dot(a_t[...], k_ref[:, at], preferred_element_type=F32)
            grads[which, pl.ds(i * 8, 8), :, at] = tile.astype(BF16).reshape(8, BLOCK, 256)
            return _

        lax.fori_loop(0, 4, columns, 0)

    load_k.wait()
    load_a[0].wait()
    gradient_tile(a_own, k_own, 0, 0)
    pl.semaphore_wait(barrier, 33)

    other = (rank(y, z, x, 1 - c), t)
    tok = [
        pltpu.make_async_remote_copy(
            k_hbm, k_oth, tok_send.at[4], tok_recv.at[4], device_id=other, device_id_type=MESH
        )
    ] + [
        pltpu.make_async_remote_copy(
            a_hbm.at[:, a_cols(1 - c, i)],
            a_oth.at[i],
            tok_send.at[i],
            tok_recv.at[i],
            device_id=other,
            device_id_type=MESH,
        )
        for i in range(4)
    ]
    for copy in tok:
        copy.start()
    for i in range(1, 4):
        load_a[i].wait()
        gradient_tile(a_own, k_own, 0, i)

    def pair_sums(block, sums):
        cross, own_sq, oth_sq = sums
        for r in range(0, BLOCK, 16):
            for l in range(0, COLS, 128):
                own = grads[0, block, r : r + 16, l : l + 128].astype(F32)
                oth = grads[1, block, r : r + 16, l : l + 128].astype(F32)
                p, q, s = own * oth, own * own, oth * oth
                cross = cross + (p[0:8] + p[8:16])
                own_sq = own_sq + (q[0:8] + q[8:16])
                oth_sq = oth_sq + (s[0:8] + s[8:16])
        return cross, own_sq, oth_sq

    zero = jnp.zeros((8, 128), F32)
    sums = (zero, zero, zero)
    tok[0].wait_recv()
    for i in range(4):
        tok[i + 1].wait_recv()
        gradient_tile(a_oth, k_oth, 1, i)
        sums = lax.fori_loop(8 * i, 8 * i + 8, pair_sums, sums)
    cross, own_sq, oth_sq = (jnp.sum(s) for s in sums)
    lower_sq = jnp.where(c == 0, own_sq, oth_sq)
    upper_sq = jnp.where(c == 0, oth_sq, own_sq)

    def entry(i, j):
        return (row8 == i) & (lane8 == j)

    def exchange(stage, slots, first, last, target):
        def go(k, _):
            pltpu.make_async_remote_copy(
                msg.at[stage],
                slots.at[k],
                r_send.at[stage, k],
                r_recv.at[stage, k],
                device_id=target(k),
                device_id_type=MESH,
            ).start()
            return _

        def arrive(k, total):
            pltpu.make_async_copy(slots.at[k], slots.at[k], r_recv.at[stage, k]).wait()
            return total + slots[k]

        lax.fori_loop(first, last, go, 0)
        return lax.fori_loop(first, last, arrive, msg[stage])

    def finish_exchange(stage, slots, first, last):
        def done(k, _):
            pltpu.make_async_copy(slots.at[k], slots.at[k], r_send.at[stage, k]).wait()
            return _

        lax.fori_loop(first, last, done, 0)

    msg[0] = (
        jnp.where(entry(0, 0), lower_sq, 0.0)
        + jnp.where(entry(1, 1), upper_sq, 0.0)
        + jnp.where(entry(0, 1) | entry(1, 0), cross, 0.0)
    )
    gram = exchange(0, slots0, 1, 4, group16)
    weight, bound = solve(gram, 2)
    scale = TOP * lax.rsqrt(bound)
    inverse1 = (1.0 / scale)
    w_low, w_up = scalars(weight * scale, 2)
    w_own = jnp.where(c == 0, w_low, w_up)
    w_oth = jnp.where(c == 0, w_up, w_low)

    def x_copy(d, b):
        return pltpu.make_async_remote_copy(
            enc_x.at[d - 1, b],
            recv_x.at[d - 1, b],
            x_send.at[d - 1, b],
            x_recv.at[d - 1, b],
            device_id=(rank(y, z, (x + d) % 4, c), t),
            device_id_type=MESH,
        )

    def x_send_block(b, _):
        for d in (2, 1, 3):
            block = b * 4 + (x + d) % 4
            for r in range(0, BLOCK, 16):
                for l in range(0, COLS, 256):
                    own = grads[0, block, r : r + 16, l : l + 256].astype(F32)
                    oth = grads[1, block, r : r + 16, l : l + 256].astype(F32)
                    enc_x[d - 1, b, r : r + 16, l : l + 256] = encode(w_own * own + w_oth * oth)
            x_copy(d, b).start()
        return _

    lax.fori_loop(0, 8, x_send_block, 0)

    def x_own_block(b, _):
        for r in range(0, BLOCK, 16):
            for l in range(0, COLS, 256):
                own = grads[0, b * 4 + x, r : r + 16, l : l + 256].astype(F32)
                oth = grads[1, b * 4 + x, r : r + 16, l : l + 256].astype(F32)
                dec_x[x, b, r : r + 16, l : l + 256] = w_own * own + w_oth * oth
        return _

    lax.fori_loop(0, 8, x_own_block, 0)
    pairs4 = [(i, j) for i in range(4) for j in range(i, 4)]

    def x_recv_block(b, sums):
        for d in (1, 3, 2):
            x_copy(d, b).wait_recv()
            source = (x + 4 - d) % 4
            for r in range(0, BLOCK, 16):
                for l in range(0, COLS, 256):
                    dec_x[source, b, r : r + 16, l : l + 256] = decode(
                        recv_x[d - 1, b, r : r + 16, l : l + 256]
                    )
        sums = list(sums)
        for r in range(0, BLOCK, 8):
            for l in range(0, COLS, 128):
                v = [dec_x[i, b, r : r + 8, l : l + 128] for i in range(4)]
                for n, (i, j) in enumerate(pairs4):
                    sums[n] = sums[n] + v[i] * v[j]
        return tuple(sums)

    sums = lax.fori_loop(0, 8, x_recv_block, (zero,) * 10)
    gram = jnp.where(entry(4, x), 0.25 * inverse1, 0.0)
    for (i, j), s in zip(pairs4, sums):
        gram = gram + jnp.where(entry(i, j) | entry(j, i), jnp.sum(s), 0.0)
    msg[1] = gram
    gram = exchange(1, slots1, 1, 16, group16)
    inv_row = jnp.where(lane8[0:1] < 4, gram[4:5], 0.0)
    inv_col = jnp.sum(jnp.where(row8 == lane8, inv_row, 0.0), axis=1, keepdims=True)
    gram = jnp.where((row8 < 4) & (lane8 < 4), gram, 0.0) * inv_row * inv_col
    weight, bound = solve(gram, 4)
    scale = TOP * lax.rsqrt(bound)
    inverse3 = (1.0 / scale)
    w_x = scalars(weight * inv_col * scale, 4)

    def y_stays(yy, half):
        py = 2 * c + yy
        return (py == y) & (half == c)

    def y_copy(yy, half, zt):
        return pltpu.make_async_remote_copy(
            enc_y.at[yy, half, zt],
            recv_y.at[y, zt],
            y_send.at[yy, half, zt],
            y_recv.at[y, zt],
            device_id=(rank(2 * c + yy, z, x, half), t),
            device_id_type=MESH,
        )

    def y_send_block(n, _):
        zt = (z + 1 + n // 2) % 4
        yy = n % 2
        b = yy * 4 + zt
        for half in range(2):
            for l in range(0, 512, 128):
                parts = []
                for first in (l, 512 + l):
                    v = [
                        dec_x[i, b, 40 * half : 40 * half + 40, first : first + 128] for i in range(4)
                    ]
                    parts.append((w_x[0] * v[0] + w_x[1] * v[1]) + (w_x[2] * v[2] + w_x[3] * v[3]))
                enc_y[yy, half, zt, :, l : l + 128] = encode(jnp.concatenate(parts, axis=0))
            here = y_stays(yy, half)

            @pl.when(here)
            def keep():
                pltpu.make_async_copy(
                    enc_y.at[yy, half, zt], recv_y.at[y, zt], y_recv.at[y, zt]
                ).start()

            @pl.when(jnp.logical_not(here))
            def push():
                y_copy(yy, half, zt).start()

        return _

    lax.fori_loop(0, 8, y_send_block, 0)

    def z_copy(d, sy):
        zt = (z + d) % 4
        return pltpu.make_async_remote_copy(
            recv_y.at[sy, zt],
            recv_z.at[z, sy],
            z_send.at[d - 1, sy],
            z_recv.at[z, sy],
            device_id=(rank(y, zt, x, c), t),
            device_id_type=MESH,
        )

    def y_arrival(sy, zt):
        pltpu.make_async_copy(recv_y.at[sy, zt], recv_y.at[sy, zt], y_recv.at[sy, zt]).wait()

    def z_relay(n, _):
        d = 1 + n // 4
        sy = n % 4
        y_arrival(sy, (z + d) % 4)
        z_copy(d, sy).start()
        return _

    lax.fori_loop(0, 12, z_relay, 0)

    def own_z(sy, _):
        y_arrival(sy, z)
        for r in range(0, BLOCK, 16):
            dec_z[sy * 4 + z, r : r + 16, :] = decode(recv_y[sy, z, r : r + 16, :])
        return _

    lax.fori_loop(0, 4, own_z, 0)

    def z_arrival(n, _):
        source = (z + 1 + n // 4) % 4
        sy = n % 4
        pltpu.make_async_copy(
            recv_z.at[source, sy], recv_z.at[source, sy], z_recv.at[source, sy]
        ).wait()
        for r in range(0, BLOCK, 16):
            dec_z[sy * 4 + source, r : r + 16, :] = decode(recv_z[source, sy, r : r + 16, :])
        return _

    lax.fori_loop(0, 12, z_arrival, 0)

    for bi in range(0, 16, 4):
        for bj in range(bi, 16, 4):
            pairs = [(i, j) for i in range(bi, bi + 4) for j in range(bj, bj + 4) if i <= j]

            def products(n, sums):
                r = pl.ds(pl.multiple_of(n * 8, 8), 8)
                sums = list(sums)
                for l in range(0, 512, 128):
                    v = {i: dec_z[i, r, l : l + 128] for i in {i for p in pairs for i in p}}
                    for m, (i, j) in enumerate(pairs):
                        sums[m] = sums[m] + v[i] * v[j]
                return tuple(sums)

            sums = lax.fori_loop(0, 10, products, (zero,) * len(pairs))
            for (i, j), s in zip(pairs, sums):
                line = jnp.sum(s, axis=0, keepdims=True)
                rows_s[i, j : j + 1, :] = line
                if i != j:
                    rows_s[j, i : i + 1, :] = line
    row16, lane16 = iotas(16)
    gram = jnp.zeros((16, 128), F32)
    for i in range(16):
        gram = gram + jnp.where(lane16 == i, jnp.sum(rows_s[i], axis=1, keepdims=True), 0.0)
    msg[2] = gram[0:8] + pltpu.roll(gram[8:16], 64, 1)
    partial = exchange(2, slots2, 1, 16, group16)
    msg[3] = partial + jnp.where(entry(0, 32 + 4 * y + z), inverse3, 0.0)
    total = exchange(3, slots3, 1, 16, plane16)
    inv_row = jnp.where(lane8[0:1] < 16, pltpu.roll(total, 96, 1)[0:1], 0.0)
    inv_col = jnp.sum(jnp.where(row16 == lane16, inv_row, 0.0), axis=1, keepdims=True)
    gram = jnp.concatenate([total, pltpu.roll(total, 64, 1)], axis=0)
    gram = jnp.where(lane16 < 16, gram, 0.0) * inv_row * inv_col
    weight, _ = solve(gram, 16)
    w_z = scalars(weight * inv_col, 16)
    for h in range(2):
        for r in range(0, 40, 8):
            for l in range(0, 512, 128):
                out = w_z[0] * dec_z[0, 40 * h + r : 40 * h + r + 8, l : l + 128]
                for i in range(1, 16):
                    out = out + w_z[i] * dec_z[i, 40 * h + r : 40 * h + r + 8, l : l + 128]
                o_ref[r : r + 8, 512 * h + l : 512 * h + l + 128] = out

    for copy in tok:
        copy.wait_send()

    def x_done(b, _):
        for d in (1, 2, 3):
            x_copy(d, b).wait_send()
        return _

    lax.fori_loop(0, 8, x_done, 0)

    def y_done(n, _):
        for half in range(2):

            @pl.when(jnp.logical_not(y_stays(n % 2, half)))
            def settle():
                y_copy(n % 2, half, n // 2).wait_send()

        return _

    lax.fori_loop(0, 8, y_done, 0)

    def z_done(n, _):
        z_copy(1 + n // 4, n % 4).wait_send()
        return _

    lax.fori_loop(0, 12, z_done, 0)
    finish_exchange(0, slots0, 1, 4)
    finish_exchange(1, slots1, 1, 16)
    finish_exchange(2, slots2, 1, 16)
    finish_exchange(3, slots3, 1, 16)


def body(activations, kv_cotangents):
    tokens = activations.shape[0]
    kv = kv_cotangents.reshape(tokens, COLS)
    dma = pltpu.SemaphoreType.DMA
    out = pl.pallas_call(
        kernel,
        out_shape=jax.ShapeDtypeStruct((40, COLS), F32),
        in_specs=[pl.BlockSpec(memory_space=pl.ANY)] * 2,
        out_specs=pl.BlockSpec(memory_space=pltpu.VMEM),
        scratch_shapes=[
            pltpu.VMEM((4, tokens, TILE), BF16),
            pltpu.VMEM((4, tokens, TILE), BF16),
            pltpu.VMEM((tokens, COLS), BF16),
            pltpu.VMEM((tokens, COLS), BF16),
            pltpu.VMEM((TILE, tokens), BF16),
            pltpu.VMEM((2, 32, BLOCK, COLS), BF16),
            pltpu.VMEM((3, 8, BLOCK, COLS), BF16),
            pltpu.VMEM((3, 8, BLOCK, COLS), BF16),
            pltpu.VMEM((4, 8, BLOCK, COLS), F32),
            pltpu.VMEM((2, 2, 4, BLOCK, 512), BF16),
            pltpu.VMEM((4, 4, BLOCK, 512), BF16),
            pltpu.VMEM((4, 4, BLOCK, 512), BF16),
            pltpu.VMEM((16, BLOCK, 512), F32),
            pltpu.VMEM((16, 16, 128), F32),
            pltpu.VMEM((4, 8, 128), F32),
            pltpu.VMEM((4, 8, 128), F32),
            pltpu.VMEM((16, 8, 128), F32),
            pltpu.VMEM((16, 8, 128), F32),
            pltpu.VMEM((16, 8, 128), F32),
            dma((5,)),
            dma((5,)),
            dma((5,)),
            dma((3, 8)),
            dma((3, 8)),
            dma((2, 2, 4)),
            dma((4, 4)),
            dma((3, 4)),
            dma((4, 4)),
            dma((4, 16)),
            dma((4, 16)),
        ],
        compiler_params=pltpu.CompilerParams(
            collective_id=0, has_side_effects=True, vmem_limit_bytes=58 * 2**20
        ),
    )(activations, kv)
    return out.reshape(40, kv_cotangents.shape[1], kv_cotangents.shape[2])


def solution(mesh):
    return jax.shard_map(
        body,
        mesh=mesh,
        in_specs=(P("dp", None), P("dp", "tensor", None)),
        out_specs=P("dp", "tensor", None),
        check_vma=False,
    )
```

time: 900 us -> 154 us (0.17)
  blocking collectives: 522 us -> 0 us
  waiting for transfers between devices: 253 us -> 0 us
  Pallas kernels: 0 us -> 149 us
  other arithmetic: 47.4 us -> 0 us
  between operations: 35.6 us -> 0.01 us
  local copies, waits for them, and re-layouts: 24.2 us -> 4.1 us
    psum x7 -> x0, blocking collectives: 522 us -> none  [group_sums(): lax.psum(partials[:, None] * group_mask[None, :], ('dp', 'tensor'))]
    ppermute x7 -> x0, waiting for transfers between devices: 253 us -> none  [swapped(): return lax.ppermute(block, axis, route)]
    pallas_call x0 -> x1, Pallas kernels: none -> 149 us  [body(): pl.pallas_call(kernel, out_shape=jax.ShapeDtypeStruct((40, COLS), F32), i...]
    reduce_sum x13 -> x0, other arithmetic: 23.9 us -> none  [the longest x7 23.3 us: merge_level(): cross_sum = jnp.sum(kept_part * received)]
    add x7 -> x0, other arithmetic: 17.9 us -> none  [merge_level(): return own_coef * kept_part + other_coef * received]
    squeeze x7 -> x0, local copies, waits for them, and re-layouts: 9.52 us -> none  [the longest x6 5.96 us: body(): lax.dynamic_index_in_dim(halves_view, 1 - level_bit, 1, keepdims=False)]
  transfers between devices with their start and end apart: 7 -> 0, of which waited for: 7 -> 0; matrix products, arithmetic and copies ran while one was open for 0% -> 0% of each run, Pallas kernels for 0% -> 0%
where the time goes in v1:
time: 154 us
  Pallas kernels  149 us (97%)
  local copies, waits for them, and re-layouts  4.1 us (3%)
    pallas_call x1, Pallas kernels, body(): pl.pallas_call(kernel, out_shape=jax.ShapeDtypeStruct((40, COLS), F32), i...  149 us

profile of v1, /device:TPU:1, one launch (start us, length us, event | category | flops | bytes accessed | tf_op | source)
XLA Modules:
  0.0 153.5 jit_solution(9164412873769715324)
XLA Ops:
  0.0 2.4 %copy.3 = bf16[64,8,4,256]{3,1,2,0:T(8,128)(2,1)} copy(bf16[64,8,4,256]{3,2,1,0:T(4,128)(2,1)} %bitcast.3) | data formatting | bytes 2097152
  2.4 149.4 %shard_map.28 = f32[40,1024]{1,0:T(8,128)} custom-call(bf16[512,5120]{1,0:T(8,128)(2,1)} %a_hbm.1, bf16[512,1024]{1,0:T(8,128)(2,1)} %bitcast.2), custom_call_target="tpu_custom_call" | custom-call | tf_op jit(solution)/shard_map/pallas_call | solution.py:480
  151.9 1.7 %reshape.7 = f32[40,4,256]{2,1,0:T(4,128)} reshape(f32[40,1024]{1,0:T(8,128)} %shard_map.28) | data formatting | bytes 327680 | tf_op jit(solution)/shard_map/reshape | solution.py:521

commit v2 on v1

--- a/solution.py
+++ b/solution.py
@@ -70,7 +70,6 @@
     rows = gram.shape[0]
     row, lane = iotas(rows)
     on_diag = row == lane
-    first_diag = jnp.sum(jnp.where(on_diag, gram, 0.0), axis=1, keepdims=True)
     weight = jnp.ones((rows, 1), F32)
     bit = 1
     while bit < count:
@@ -89,18 +88,47 @@
             gram = gram + partner_rows(gram, bit)
             gram = gram + partner_lanes(gram, bit)
         bit *= 2
-    bound = float(count) * jnp.sum(weight * weight * first_diag, axis=0, keepdims=True) + 1e-36
+    return weight
+
+
+def total(values):
+    return jnp.sum(values, keepdims=True)
+
+
+def wide(value, rows=16):
+    return jnp.broadcast_to(value, (rows, 128))
+
+
+def fold(values):
+    rows, columns = values.shape
+    parts = [
+        values[r : r + 8, l : l + 128] for r in range(0, rows, 8) for l in range(0, columns, 128)
+    ]
+    while len(parts) > 1:
+        odd = parts[len(parts) & ~1 :]
+        parts = [p + q for p, q in zip(parts[0::2], parts[1::2])] + odd
+    return parts[0]
+
+
+def pair_weights(low_sq, up_sq, cross):
+    return 1.0 - cross / (2.0 * low_sq + EPS), 1.0 - cross / (2.0 * up_sq + EPS)
+
+
+def solve4(gram):
+    c0, c1 = pair_weights(gram[0, 0], gram[1, 1], gram[0, 1])
+    c2, c3 = pair_weights(gram[2, 2], gram[3, 3], gram[2, 3])
+    low_sq = c0 * c0 * gram[0, 0] + 2.0 * c0 * c1 * gram[0, 1] + c1 * c1 * gram[1, 1]
+    up_sq = c2 * c2 * gram[2, 2] + 2.0 * c2 * c3 * gram[2, 3] + c3 * c3 * gram[3, 3]
+    cross = c0 * (c2 * gram[0, 2] + c3 * gram[0, 3]) + c1 * (c2 * gram[1, 2] + c3 * gram[1, 3])
+    low, up = pair_weights(low_sq, up_sq, cross)
+    weight = [c0 * low, c1 * low, c2 * up, c3 * up]
+    bound = sum(weight[i] * weight[i] * gram[i, i] for i in range(4)) * 4.0 + 1e-36
     return weight, bound
-
-
-def scalars(column, count):
-    row = lax.broadcasted_iota(jnp.int32, column.shape, 0)
-    return [jnp.sum(jnp.where(row == i, column, 0.0)) for i in range(count)]
 
 
 def kernel(
     a_hbm, k_hbm, o_ref,
-    a_own, a_oth, k_own, k_oth, a_t, grads, enc_x, recv_x, dec_x, enc_y, recv_y, recv_z, dec_z,
+    a_own, a_oth, k_raw, k_own, k_oth, grads, enc_x, recv_x, dec_x, enc_y, recv_y, recv_z, dec_z,
     rows_s, msg, slots0, slots1, slots2, slots3,
     load_sem, tok_send, tok_recv, x_send, x_recv, y_send, y_recv, z_send, z_recv, r_send, r_recv,
 ):
@@ -134,41 +162,28 @@
     def a_cols(core, i):
         return pl.ds(pl.multiple_of(core * HALF + i * TILE, 128), TILE)
 
-    load_k = pltpu.make_async_copy(k_hbm, k_own, load_sem.at[4])
+    load_k = pltpu.make_async_copy(k_hbm, k_raw, load_sem.at[4])
     load_k.start()
-    load_a = [
-        pltpu.make_async_copy(a_hbm.at[:, a_cols(c, i)], a_own.at[i], load_sem.at[i])
-        for i in range(4)
-    ]
-    for copy in load_a:
-        copy.start()
+
+    def load_a(i):
+        return pltpu.make_async_copy(a_hbm.at[:, a_cols(c, i)], a_own.at[i], load_sem.at[i])
+
+    def start_load(i, _):
+        load_a(i).start()
+        return _
+
+    lax.fori_loop(0, 4, start_load, 0)
     lax.fori_loop(1, 16, greet_group, 0)
     lax.fori_loop(1, 16, greet_plane, 0)
     lax.fori_loop(1, 4, greet_other, 0)
-
-    def gradient_tile(a_ref, k_ref, which, i):
-        a_t[...] = a_ref[i].T
-
-        def columns(n, _):
-            at = pl.ds(pl.multiple_of(n * 256, 256), 256)
-            tile = jnp.dot(a_t[...], k_ref[:, at], preferred_element_type=F32)
-            grads[which, pl.ds(i * 8, 8), :, at] = tile.astype(BF16).reshape(8, BLOCK, 256)
-            return _
-
-        lax.fori_loop(0, 4, columns, 0)
-
-    load_k.wait()
-    load_a[0].wait()
-    gradient_tile(a_own, k_own, 0, 0)
     pl.semaphore_wait(barrier, 33)
-
     other = (rank(y, z, x, 1 - c), t)
-    tok = [
-        pltpu.make_async_remote_copy(
-            k_hbm, k_oth, tok_send.at[4], tok_recv.at[4], device_id=other, device_id_type=MESH
-        )
-    ] + [
-        pltpu.make_async_remote_copy(
+    give_k = pltpu.make_async_remote_copy(
+        k_own, k_oth, tok_send.at[4], tok_recv.at[4], device_id=other, device_id_type=MESH
+    )
+
+    def give_a(i):
+        return pltpu.make_async_remote_copy(
             a_hbm.at[:, a_cols(1 - c, i)],
             a_oth.at[i],
             tok_send.at[i],
@@ -176,34 +191,51 @@
             device_id=other,
             device_id_type=MESH,
         )
-        for i in range(4)
-    ]
-    for copy in tok:
-        copy.start()
-    for i in range(1, 4):
-        load_a[i].wait()
-        gradient_tile(a_own, k_own, 0, i)
-
-    def pair_sums(block, sums):
-        cross, own_sq, oth_sq = sums
-        for r in range(0, BLOCK, 16):
-            for l in range(0, COLS, 128):
-                own = grads[0, block, r : r + 16, l : l + 128].astype(F32)
-                oth = grads[1, block, r : r + 16, l : l + 128].astype(F32)
-                p, q, s = own * oth, own * own, oth * oth
-                cross = cross + (p[0:8] + p[8:16])
-                own_sq = own_sq + (q[0:8] + q[8:16])
-                oth_sq = oth_sq + (s[0:8] + s[8:16])
-        return cross, own_sq, oth_sq
+
+    give_a(0).start()
+    load_k.wait()
+
+    def pack_k(n, _):
+        r = pl.ds(pl.multiple_of(n * 32, 32), 32)
+        k_own[r] = pltpu.einshape("thc->t(hc)", k_raw[r])
+        return _
+
+    lax.fori_loop(0, k_raw.shape[0] // 32, pack_k, 0)
+    give_k.start()
+
+    def start_give(i, _):
+        give_a(i).start()
+        return _
+
+    lax.fori_loop(1, 4, start_give, 0)
+
+    def gradient(a_ref, k_ref):
+        return lax.dot_general(
+            a_ref[...], k_ref[...], (((0,), (0,)), ((), ())), preferred_element_type=F32
+        ).astype(BF16)
+
+    def own_tile(i, own_sq):
+        load_a(i).wait()
+        tile = gradient(a_own.at[i], k_own)
+        grads[0, pl.ds(i * 8, 8)] = tile.reshape(8, BLOCK, COLS)
+        tile = tile.astype(F32)
+        return own_sq + fold(tile * tile)
 
     zero = jnp.zeros((8, 128), F32)
-    sums = (zero, zero, zero)
-    tok[0].wait_recv()
-    for i in range(4):
-        tok[i + 1].wait_recv()
-        gradient_tile(a_oth, k_oth, 1, i)
-        sums = lax.fori_loop(8 * i, 8 * i + 8, pair_sums, sums)
-    cross, own_sq, oth_sq = (jnp.sum(s) for s in sums)
+    own_sq = lax.fori_loop(0, 4, own_tile, zero)
+    give_k.wait_recv()
+
+    def other_tile(i, sums):
+        cross, oth_sq = sums
+        give_a(i).wait_recv()
+        tile = gradient(a_oth.at[i], k_oth)
+        grads[1, pl.ds(i * 8, 8)] = tile.reshape(8, BLOCK, COLS)
+        tile = tile.astype(F32)
+        own = grads[0, pl.ds(i * 8, 8)].astype(F32).reshape(TILE, COLS)
+        return cross + fold(own * tile), oth_sq + fold(tile * tile)
+
+    cross, oth_sq = lax.fori_loop(0, 4, other_tile, (zero, zero))
+    own_sq, oth_sq, cross = total(own_sq), total(oth_sq), total(cross)
     lower_sq = jnp.where(c == 0, own_sq, oth_sq)
     upper_sq = jnp.where(c == 0, oth_sq, own_sq)
 
@@ -222,9 +254,9 @@
             ).start()
             return _
 
-        def arrive(k, total):
+        def arrive(k, table):
             pltpu.make_async_copy(slots.at[k], slots.at[k], r_recv.at[stage, k]).wait()
-            return total + slots[k]
+            return table + slots[k]
 
         lax.fori_loop(first, last, go, 0)
         return lax.fori_loop(first, last, arrive, msg[stage])
@@ -242,12 +274,22 @@
         + jnp.where(entry(0, 1) | entry(1, 0), cross, 0.0)
     )
     gram = exchange(0, slots0, 1, 4, group16)
-    weight, bound = solve(gram, 2)
+
+    def pick(table, i, j):
+        return total(jnp.where(entry(i, j), table, 0.0))
+
+    lower_sq, upper_sq, cross = pick(gram, 0, 0), pick(gram, 1, 1), pick(gram, 0, 1)
+    w_low, w_up = pair_weights(lower_sq, upper_sq, cross)
+    bound = 2.0 * (w_low * w_low * lower_sq + w_up * w_up * upper_sq) + 1e-36
     scale = TOP * lax.rsqrt(bound)
-    inverse1 = (1.0 / scale)
-    w_low, w_up = scalars(weight * scale, 2)
-    w_own = jnp.where(c == 0, w_low, w_up)
-    w_oth = jnp.where(c == 0, w_up, w_low)
+    inverse1 = 1.0 / scale
+    w_own = wide(scale * jnp.where(c == 0, w_low, w_up))
+    w_oth = wide(scale * jnp.where(c == 0, w_up, w_low))
+
+    def pair_of(block, r, l):
+        own = grads[0, block, r : r + 16, l : l + 128].astype(F32)
+        oth = grads[1, block, r : r + 16, l : l + 128].astype(F32)
+        return w_own * own + w_oth * oth
 
     def x_copy(d, b):
         return pltpu.make_async_remote_copy(
@@ -263,10 +305,8 @@
         for d in (2, 1, 3):
             block = b * 4 + (x + d) % 4
             for r in range(0, BLOCK, 16):
-                for l in range(0, COLS, 256):
-                    own = grads[0, block, r : r + 16, l : l + 256].astype(F32)
-                    oth = grads[1, block, r : r + 16, l : l + 256].astype(F32)
-                    enc_x[d - 1, b, r : r + 16, l : l + 256] = encode(w_own * own + w_oth * oth)
+                for l in range(0, COLS, 128):
+                    enc_x[d - 1, b, r : r + 16, l : l + 128] = encode(pair_of(block, r, l))
             x_copy(d, b).start()
         return _
 
@@ -274,10 +314,8 @@
 
     def x_own_block(b, _):
         for r in range(0, BLOCK, 16):
-            for l in range(0, COLS, 256):
-                own = grads[0, b * 4 + x, r : r + 16, l : l + 256].astype(F32)
-                oth = grads[1, b * 4 + x, r : r + 16, l : l + 256].astype(F32)
-                dec_x[x, b, r : r + 16, l : l + 256] = w_own * own + w_oth * oth
+            for l in range(0, COLS, 128):
+                dec_x[x, b, r : r + 16, l : l + 128] = pair_of(b * 4 + x, r, l)
         return _
 
     lax.fori_loop(0, 8, x_own_block, 0)
@@ -301,18 +339,16 @@
         return tuple(sums)
 
     sums = lax.fori_loop(0, 8, x_recv_block, (zero,) * 10)
-    gram = jnp.where(entry(4, x), 0.25 * inverse1, 0.0)
+    table = jnp.where(entry(4, x), 0.25 * inverse1, 0.0)
     for (i, j), s in zip(pairs4, sums):
-        gram = gram + jnp.where(entry(i, j) | entry(j, i), jnp.sum(s), 0.0)
-    msg[1] = gram
-    gram = exchange(1, slots1, 1, 16, group16)
-    inv_row = jnp.where(lane8[0:1] < 4, gram[4:5], 0.0)
-    inv_col = jnp.sum(jnp.where(row8 == lane8, inv_row, 0.0), axis=1, keepdims=True)
-    gram = jnp.where((row8 < 4) & (lane8 < 4), gram, 0.0) * inv_row * inv_col
-    weight, bound = solve(gram, 4)
+        table = table + jnp.where(entry(i, j), total(s), 0.0)
+    msg[1] = table
+    table = exchange(1, slots1, 1, 16, group16)
+    inv = [pick(table, 4, i) for i in range(4)]
+    weight, bound = solve4({(i, j): pick(table, i, j) * inv[i] * inv[j] for i, j in pairs4})
     scale = TOP * lax.rsqrt(bound)
-    inverse3 = (1.0 / scale)
-    w_x = scalars(weight * inv_col * scale, 4)
+    inverse3 = 1.0 / scale
+    w_x = [wide(weight[i] * inv[i] * scale, 40) for i in range(4)]
 
     def y_stays(yy, half):
         py = 2 * c + yy
@@ -426,13 +462,13 @@
     msg[2] = gram[0:8] + pltpu.roll(gram[8:16], 64, 1)
     partial = exchange(2, slots2, 1, 16, group16)
     msg[3] = partial + jnp.where(entry(0, 32 + 4 * y + z), inverse3, 0.0)
-    total = exchange(3, slots3, 1, 16, plane16)
-    inv_row = jnp.where(lane8[0:1] < 16, pltpu.roll(total, 96, 1)[0:1], 0.0)
+    table = exchange(3, slots3, 1, 16, plane16)
+    inv_row = jnp.where(lane8[0:1] < 16, pltpu.roll(table, 96, 1)[0:1], 0.0)
     inv_col = jnp.sum(jnp.where(row16 == lane16, inv_row, 0.0), axis=1, keepdims=True)
-    gram = jnp.concatenate([total, pltpu.roll(total, 64, 1)], axis=0)
+    gram = jnp.concatenate([table, pltpu.roll(table, 64, 1)], axis=0)
     gram = jnp.where(lane16 < 16, gram, 0.0) * inv_row * inv_col
-    weight, _ = solve(gram, 16)
-    w_z = scalars(weight * inv_col, 16)
+    weight = solve(gram, 16) * inv_col
+    w_z = [wide(weight[i : i + 1], 8) for i in range(16)]
     for h in range(2):
         for r in range(0, 40, 8):
             for l in range(0, 512, 128):
@@ -441,8 +477,13 @@
                     out = out + w_z[i] * dec_z[i, 40 * h + r : 40 * h + r + 8, l : l + 128]
                 o_ref[r : r + 8, 512 * h + l : 512 * h + l + 128] = out
 
-    for copy in tok:
-        copy.wait_send()
+    give_k.wait_send()
+
+    def given(i, _):
+        give_a(i).wait_send()
+        return _
+
+    lax.fori_loop(0, 4, given, 0)
 
     def x_done(b, _):
         for d in (1, 2, 3):
@@ -475,7 +516,6 @@
 
 def body(activations, kv_cotangents):
     tokens = activations.shape[0]
-    kv = kv_cotangents.reshape(tokens, COLS)
     dma = pltpu.SemaphoreType.DMA
     out = pl.pallas_call(
         kernel,
@@ -485,9 +525,9 @@
         scratch_shapes=[
             pltpu.VMEM((4, tokens, TILE), BF16),
             pltpu.VMEM((4, tokens, TILE), BF16),
+            pltpu.VMEM(kv_cotangents.shape, BF16),
             pltpu.VMEM((tokens, COLS), BF16),
             pltpu.VMEM((tokens, COLS), BF16),
-            pltpu.VMEM((TILE, tokens), BF16),
             pltpu.VMEM((2, 32, BLOCK, COLS), BF16),
             pltpu.VMEM((3, 8, BLOCK, COLS), BF16),
             pltpu.VMEM((3, 8, BLOCK, COLS), BF16),
@@ -517,7 +557,7 @@
         compiler_params=pltpu.CompilerParams(
             collective_id=0, has_side_effects=True, vmem_limit_bytes=58 * 2**20
         ),
-    )(activations, kv)
+    )(activations, kv_cotangents)
     return out.reshape(40, kv_cotangents.shape[1], kv_cotangents.shape[2])
 
 

time: 154 us -> 146 us (0.948)
  Pallas kernels: 149 us -> 144 us
  local copies, waits for them, and re-layouts: 4.1 us -> 1.66 us
    pallas_call x1, Pallas kernels: 149 us -> 144 us  [body(): pl.pallas_call(kernel, out_shape=jax.ShapeDtypeStruct((40, COLS), F32), i...]
    unnamed x1 -> x0, local copies, waits for them, and re-layouts: 2.44 us -> none
where the time goes in v2:
time: 146 us
  Pallas kernels  144 us (99%)
  local copies, waits for them, and re-layouts  1.66 us (1%)
    pallas_call x1, Pallas kernels, body(): pl.pallas_call(kernel, out_shape=jax.ShapeDtypeStruct((40, COLS), F32), i...  144 us

profile of v2, /device:TPU:1, one launch (start us, length us, event | category | flops | bytes accessed | tf_op | source)
XLA Modules:
  0.0 145.7 jit_solution(6909619280502840473)
XLA Ops:
  0.0 144.0 %shard_map.28 = f32[40,1024]{1,0:T(8,128)} custom-call(bf16[512,5120]{1,0:T(8,128)(2,1)} %a_hbm.1, bf16[512,4,256]{2,1,0:T(4,128)(2,1)} %k_hbm.1), custom_call_target="tpu_custom_call" | custom-call | tf_op jit(solution)/shard_map/pallas_call | solution.py:520
  144.0 1.7 %reshape.3 = f32[40,4,256]{2,1,0:T(4,128)} reshape(f32[40,1024]{1,0:T(8,128)} %shard_map.28) | data formatting | bytes 327680 | tf_op jit(solution)/shard_map/reshape | solution.py:561

commit v3 on v2

--- a/solution.py
+++ b/solution.py
@@ -17,6 +17,7 @@
 TILE = 640
 BLOCK = 80
 COLS = 1024
+PART = 512
 
 
 def coords(dp):
@@ -128,9 +129,11 @@
 
 def kernel(
     a_hbm, k_hbm, o_ref,
-    a_own, a_oth, k_raw, k_own, k_oth, grads, enc_x, recv_x, dec_x, enc_y, recv_y, recv_z, dec_z,
-    rows_s, msg, slots0, slots1, slots2, slots3,
-    load_sem, tok_send, tok_recv, x_send, x_recv, y_send, y_recv, z_send, z_recv, r_send, r_recv,
+    a_own, a_oth, k_raw, k_own, k_oth, grads, enc_x, recv_x, dec_x, enc_q, recv_q, recv_r, dec_q, sums_q,
+    enc_y, recv_y, recv_z, enc_yq, recv_yq, dec_z,
+    rows_s, msg, msg_q, slots0, slots1, slots2, slots3, slots_q, slots_w,
+    load_sem, tok_send, tok_recv, x_send, x_recv, zq_send, zq_recv, xr_send, xr_recv,
+    yq_send, yq_recv, y_send, y_recv, z_send, z_recv, r_send, r_recv, q_sems,
 ):
     me = lax.axis_index("dp")
     t = lax.axis_index("tensor")
@@ -291,30 +294,85 @@
         oth = grads[1, block, r : r + 16, l : l + 128].astype(F32)
         return w_own * own + w_oth * oth
 
+    def along_x(d):
+        return rank(y, z, (x + d) % 4, c), t
+
+    def along_z(d):
+        return rank(y, (z + d) % 4, x, c), t
+
     def x_copy(d, b):
         return pltpu.make_async_remote_copy(
             enc_x.at[d - 1, b],
             recv_x.at[d - 1, b],
             x_send.at[d - 1, b],
             x_recv.at[d - 1, b],
-            device_id=(rank(y, z, (x + d) % 4, c), t),
+            device_id=along_x(d),
             device_id_type=MESH,
         )
 
-    def x_send_block(b, _):
+    def zq_copy(dz, yy, dx):
+        return pltpu.make_async_remote_copy(
+            enc_q.at[dz - 1, yy, dx],
+            recv_q.at[dz, yy, dx],
+            zq_send.at[dz - 1, yy * 4 + dx],
+            zq_recv.at[dz - 1, yy * 4 + dx],
+            device_id=along_z(dz),
+            device_id_type=MESH,
+        )
+
+    def xr_copy(dx, dz, yy):
+        return pltpu.make_async_remote_copy(
+            recv_q.at[dz, yy, dx],
+            recv_r.at[dx - 1, dz, yy],
+            xr_send.at[dx - 1, dz * 2 + yy],
+            xr_recv.at[dx - 1, dz * 2 + yy],
+            device_id=along_x(dx),
+            device_id_type=MESH,
+        )
+
+    def x_send_block(b):
         for d in (2, 1, 3):
             block = b * 4 + (x + d) % 4
             for r in range(0, BLOCK, 16):
-                for l in range(0, COLS, 128):
+                for l in range(0, PART, 128):
                     enc_x[d - 1, b, r : r + 16, l : l + 128] = encode(pair_of(block, r, l))
             x_copy(d, b).start()
-        return _
-
-    lax.fori_loop(0, 8, x_send_block, 0)
+
+    def q_send_block(yy, dx):
+        for dz in (2, 1, 3, 0):
+            block = yy * 16 + ((z + dz) % 4) * 4 + (x + dx) % 4
+            for r in range(0, BLOCK, 16):
+                for l in range(0, COLS - PART, 128):
+                    code = encode(pair_of(block, r, PART + l))
+                    if dz:
+                        enc_q[dz - 1, yy, dx, r : r + 16, l : l + 128] = code
+                    else:
+                        recv_q[0, yy, dx, r : r + 16, l : l + 128] = code
+            if dz:
+                zq_copy(dz, yy, dx).start()
+
+    def send_far(m, _):
+        x_send_block(m)
+        q_send_block(m, 2)
+        return _
+
+    def send_near(k, _):
+        x_send_block(2 + k)
+        q_send_block(k // 2, 1 + 2 * (k % 2))
+        return _
+
+    def send_own(m, _):
+        x_send_block(6 + m)
+        q_send_block(m, 0)
+        return _
+
+    lax.fori_loop(0, 2, send_far, 0)
+    lax.fori_loop(0, 4, send_near, 0)
+    lax.fori_loop(0, 2, send_own, 0)
 
     def x_own_block(b, _):
         for r in range(0, BLOCK, 16):
-            for l in range(0, COLS, 128):
+            for l in range(0, PART, 128):
                 dec_x[x, b, r : r + 16, l : l + 128] = pair_of(b * 4 + x, r, l)
         return _
 
@@ -326,29 +384,132 @@
             x_copy(d, b).wait_recv()
             source = (x + 4 - d) % 4
             for r in range(0, BLOCK, 16):
-                for l in range(0, COLS, 256):
+                for l in range(0, PART, 256):
                     dec_x[source, b, r : r + 16, l : l + 256] = decode(
                         recv_x[d - 1, b, r : r + 16, l : l + 256]
                     )
         sums = list(sums)
         for r in range(0, BLOCK, 8):
-            for l in range(0, COLS, 128):
+            for l in range(0, PART, 128):
                 v = [dec_x[i, b, r : r + 8, l : l + 128] for i in range(4)]
                 for n, (i, j) in enumerate(pairs4):
                     sums[n] = sums[n] + v[i] * v[j]
         return tuple(sums)
 
-    sums = lax.fori_loop(0, 8, x_recv_block, (zero,) * 10)
+    def relay(yy, dx):
+        for dz in (0, 1, 3, 2):
+            if dz:
+                zq_copy(dz, yy, dx).wait_recv()
+            xr_copy(dx, dz, yy).start()
+
+    def relay_far(m, _):
+        relay(m, 2)
+        return _
+
+    def relay_near(k, _):
+        relay(k // 2, 1 + 2 * (k % 2))
+        return _
+
+    sums = lax.fori_loop(0, 4, x_recv_block, (zero,) * 10)
+    lax.fori_loop(0, 2, relay_far, 0)
+    sums = lax.fori_loop(4, 8, x_recv_block, sums)
+    lax.fori_loop(0, 4, relay_near, 0)
+
+    def q_decode(dx, yy):
+        def one(dz, _):
+            if dx:
+                xr_copy(dx, dz, yy).wait_recv()
+                source = recv_r.at[dx - 1, dz, yy]
+            else:
+                source = recv_q.at[dz, yy, 0]
+            for r in range(0, BLOCK, 16):
+                for l in range(0, COLS - PART, 256):
+                    dec_q[dz, (x + 4 - dx) % 4, yy, r : r + 16, l : l + 256] = decode(
+                        source[r : r + 16, l : l + 256]
+                    )
+            return _
+
+        lax.fori_loop(0, 4, one, 0)
+
+    def q_own(yy):
+        for dz in (1, 2, 3):
+            zq_copy(dz, yy, 0).wait_recv()
+        q_decode(0, yy)
+
+    def q_gram(yy):
+        def one(dz, _):
+            sums = [zero if yy == 0 else sums_q[dz, n] for n in range(10)]
+            for r in range(0, BLOCK, 8):
+                for l in range(0, COLS - PART, 128):
+                    v = [dec_q[dz, i, yy, r : r + 8, l : l + 128] for i in range(4)]
+                    for n, (i, j) in enumerate(pairs4):
+                        sums[n] = sums[n] + v[i] * v[j]
+            for n in range(10):
+                sums_q[dz, n] = sums[n]
+            return _
+
+        lax.fori_loop(0, 4, one, 0)
+
+    q_decode(2, 0)
+    q_decode(2, 1)
+    q_decode(1, 0)
+    q_decode(3, 0)
+    q_own(0)
+    q_gram(0)
+    q_decode(1, 1)
+    q_decode(3, 1)
+    q_own(1)
+    q_gram(1)
+
+    def q_copy(dz):
+        return pltpu.make_async_remote_copy(
+            msg_q.at[dz],
+            slots_q.at[dz],
+            q_sems.at[0, dz],
+            q_sems.at[1, dz],
+            device_id=along_z(4 - dz),
+            device_id_type=MESH,
+        )
+
+    def tile_of(sums):
+        table = jnp.zeros((8, 128), F32)
+        for (i, j), s in zip(pairs4, sums):
+            table = table + jnp.where(entry(i, j), total(s), 0.0)
+        return table
+
+    for dz in (2, 1, 3):
+        msg_q[dz] = tile_of([sums_q[dz, n] for n in range(10)])
+        q_copy(dz).start()
     table = jnp.where(entry(4, x), 0.25 * inverse1, 0.0)
-    for (i, j), s in zip(pairs4, sums):
-        table = table + jnp.where(entry(i, j), total(s), 0.0)
+    table = table + tile_of([s + sums_q[0, n] for n, s in enumerate(sums)])
+    for dz in (1, 3, 2):
+        q_copy(dz).wait_recv()
+        table = table + slots_q[dz]
     msg[1] = table
     table = exchange(1, slots1, 1, 16, group16)
     inv = [pick(table, 4, i) for i in range(4)]
     weight, bound = solve4({(i, j): pick(table, i, j) * inv[i] * inv[j] for i, j in pairs4})
     scale = TOP * lax.rsqrt(bound)
     inverse3 = 1.0 / scale
-    w_x = [wide(weight[i] * inv[i] * scale, 40) for i in range(4)]
+    w_own_z = [weight[i] * inv[i] * scale for i in range(4)]
+
+    def w_copy(dz):
+        return pltpu.make_async_remote_copy(
+            msg_q.at[0],
+            slots_w.at[dz],
+            q_sems.at[2, dz],
+            q_sems.at[3, dz],
+            device_id=along_z(dz),
+            device_id_type=MESH,
+        )
+
+    table = jnp.zeros((8, 128), F32)
+    for i in range(4):
+        table = table + jnp.where(entry(0, i), w_own_z[i], 0.0)
+    msg_q[0] = table
+    for dz in (2, 1, 3):
+        w_copy(dz).start()
+    w_x = [wide(w_own_z[i], 40) for i in range(4)]
 
     def y_stays(yy, half):
         py = 2 * c + yy
@@ -364,19 +525,25 @@
             device_id_type=MESH,
         )
 
+    def combined(weights, block, half, l, width):
+        parts = []
+        for first in (l, width + l):
+            rows, at = slice(40 * half, 40 * half + 40), slice(first, first + 128)
+            v = [block(i, rows, at) for i in range(4)]
+            parts.append(
+                (weights[0] * v[0] + weights[1] * v[1]) + (weights[2] * v[2] + weights[3] * v[3])
+            )
+        return encode(jnp.concatenate(parts, axis=0))
+
     def y_send_block(n, _):
         zt = (z + 1 + n // 2) % 4
         yy = n % 2
         b = yy * 4 + zt
         for half in range(2):
-            for l in range(0, 512, 128):
-                parts = []
-                for first in (l, 512 + l):
-                    v = [
-                        dec_x[i, b, 40 * half : 40 * half + 40, first : first + 128] for i in range(4)
-                    ]
-                    parts.append((w_x[0] * v[0] + w_x[1] * v[1]) + (w_x[2] * v[2] + w_x[3] * v[3]))
-                enc_y[yy, half, zt, :, l : l + 128] = encode(jnp.concatenate(parts, axis=0))
+            for l in range(0, PART // 2, 128):
+                enc_y[yy, half, zt, :, l : l + 128] = combined(
+                    w_x, lambda i, r, at: dec_x[i, b, r, at], half, l, PART // 2
+                )
             here = y_stays(yy, half)
 
             @pl.when(here)
@@ -416,13 +583,66 @@
 
     lax.fori_loop(0, 12, z_relay, 0)
 
+    def yq_copy(yy, half):
+        return pltpu.make_async_remote_copy(
+            enc_yq.at[yy, half],
+            recv_yq.at[y],
+            yq_send.at[yy, half],
+            yq_recv.at[y],
+            device_id=(rank(2 * c + yy, z, x, half), t),
+            device_id_type=MESH,
+        )
+
+    w_by_z = []
+    for dz in range(4):
+        if dz:
+            w_copy(dz).wait_recv()
+            w_by_z.append([wide(pick(slots_w[dz], 0, i), 40) for i in range(4)])
+        else:
+            w_by_z.append(w_x)
+
+    def yq_send_block(yy, _):
+        for half in range(2):
+            for dz in range(4):
+                for l in range(0, (COLS - PART) // 2, 128):
+                    enc_yq[yy, half, (z + 4 - dz) % 4, :, l : l + 128] = combined(
+                        w_by_z[dz],
+                        lambda i, r, at: dec_q[dz, i, yy, r, at],
+                        half,
+                        l,
+                        (COLS - PART) // 2,
+                    )
+            here = y_stays(yy, half)
+
+            @pl.when(here)
+            def keep():
+                pltpu.make_async_copy(enc_yq.at[yy, half], recv_yq.at[y], yq_recv.at[y]).start()
+
+            @pl.when(jnp.logical_not(here))
+            def push():
+                yq_copy(yy, half).start()
+
+        return _
+
+    lax.fori_loop(0, 2, yq_send_block, 0)
+
     def own_z(sy, _):
         y_arrival(sy, z)
         for r in range(0, BLOCK, 16):
-            dec_z[sy * 4 + z, r : r + 16, :] = decode(recv_y[sy, z, r : r + 16, :])
+            dec_z[sy * 4 + z, r : r + 16, 0 : PART // 2] = decode(recv_y[sy, z, r : r + 16, :])
         return _
 
     lax.fori_loop(0, 4, own_z, 0)
+
+    def yq_arrival(n, _):
+        sy = (y + n) % 4
+        pltpu.make_async_copy(recv_yq.at[sy], recv_yq.at[sy], yq_recv.at[sy]).wait()
+        for sz in range(4):
+            for r in range(0, BLOCK, 16):
+                dec_z[sy * 4 + sz, r : r + 16, PART // 2 :] = decode(recv_yq[sy, sz, r : r + 16, :])
+        return _
+
+    lax.fori_loop(0, 4, yq_arrival, 0)
 
     def z_arrival(n, _):
         source = (z + 1 + n // 4) % 4
@@ -431,7 +651,9 @@
             recv_z.at[source, sy], recv_z.at[source, sy], z_recv.at[source, sy]
         ).wait()
         for r in range(0, BLOCK, 16):
-            dec_z[sy * 4 + source, r : r + 16, :] = decode(recv_z[source, sy, r : r + 16, :])
+            dec_z[sy * 4 + source, r : r + 16, 0 : PART // 2] = decode(
+                recv_z[source, sy, r : r + 16, :]
+            )
         return _
 
     lax.fori_loop(0, 12, z_arrival, 0)
@@ -469,13 +691,16 @@
     gram = jnp.where(lane16 < 16, gram, 0.0) * inv_row * inv_col
     weight = solve(gram, 16) * inv_col
     w_z = [wide(weight[i : i + 1], 8) for i in range(16)]
-    for h in range(2):
-        for r in range(0, 40, 8):
-            for l in range(0, 512, 128):
-                out = w_z[0] * dec_z[0, 40 * h + r : 40 * h + r + 8, l : l + 128]
-                for i in range(1, 16):
-                    out = out + w_z[i] * dec_z[i, 40 * h + r : 40 * h + r + 8, l : l + 128]
-                o_ref[r : r + 8, 512 * h + l : 512 * h + l + 128] = out
+    for first, width, at in ((0, PART // 2, 0), (PART, (COLS - PART) // 2, PART // 2)):
+        for h in range(2):
+            for r in range(0, 40, 8):
+                for l in range(0, width, 128):
+                    rows, lanes = slice(40 * h + r, 40 * h + r + 8), slice(at + l, at + l + 128)
+                    terms = [w_z[i] * dec_z[i, rows, lanes] for i in range(16)]
+                    while len(terms) > 1:
+                        terms = [p + q for p, q in zip(terms[0::2], terms[1::2])]
+                    column = first + h * width + l
+                    o_ref[r : r + 8, column : column + 128] = terms[0]
 
     give_k.wait_send()
 
@@ -491,6 +716,34 @@
         return _
 
     lax.fori_loop(0, 8, x_done, 0)
+
+    def zq_done(n, _):
+        for dz in (1, 2, 3):
+            zq_copy(dz, n // 4, n % 4).wait_send()
+        return _
+
+    lax.fori_loop(0, 8, zq_done, 0)
+
+    def xr_done(n, _):
+        for dx in (1, 2, 3):
+            xr_copy(dx, n // 2, n % 2).wait_send()
+        return _
+
+    lax.fori_loop(0, 8, xr_done, 0)
+    for dz in (1, 2, 3):
+        q_copy(dz).wait_send()
+        w_copy(dz).wait_send()
+
+    def yq_done(yy, _):
+        for half in range(2):
+
+            @pl.when(jnp.logical_not(y_stays(yy, half)))
+            def settle_q():
+                yq_copy(yy, half).wait_send()
+
+        return _
+
+    lax.fori_loop(0, 2, yq_done, 0)
 
     def y_done(n, _):
         for half in range(2):
@@ -517,6 +770,7 @@
 def body(activations, kv_cotangents):
     tokens = activations.shape[0]
     dma = pltpu.SemaphoreType.DMA
+    rest = COLS - PART
     out = pl.pallas_call(
         kernel,
         out_shape=jax.ShapeDtypeStruct((40, COLS), F32),
@@ -529,30 +783,47 @@
             pltpu.VMEM((tokens, COLS), BF16),
             pltpu.VMEM((tokens, COLS), BF16),
             pltpu.VMEM((2, 32, BLOCK, COLS), BF16),
-            pltpu.VMEM((3, 8, BLOCK, COLS), BF16),
-            pltpu.VMEM((3, 8, BLOCK, COLS), BF16),
-            pltpu.VMEM((4, 8, BLOCK, COLS), F32),
-            pltpu.VMEM((2, 2, 4, BLOCK, 512), BF16),
-            pltpu.VMEM((4, 4, BLOCK, 512), BF16),
-            pltpu.VMEM((4, 4, BLOCK, 512), BF16),
-            pltpu.VMEM((16, BLOCK, 512), F32),
+            pltpu.VMEM((3, 8, BLOCK, PART), BF16),
+            pltpu.VMEM((3, 8, BLOCK, PART), BF16),
+            pltpu.VMEM((4, 8, BLOCK, PART), F32),
+            pltpu.VMEM((3, 2, 4, BLOCK, rest), BF16),
+            pltpu.VMEM((4, 2, 4, BLOCK, rest), BF16),
+            pltpu.VMEM((3, 4, 2, BLOCK, rest), BF16),
+            pltpu.VMEM((4, 4, 2, BLOCK, rest), F32),
+            pltpu.VMEM((4, 10, 8, 128), F32),
+            pltpu.VMEM((2, 2, 4, BLOCK, PART // 2), BF16),
+            pltpu.VMEM((4, 4, BLOCK, PART // 2), BF16),
+            pltpu.VMEM((4, 4, BLOCK, PART // 2), BF16),
+            pltpu.VMEM((2, 2, 4, BLOCK, rest // 2), BF16),
+            pltpu.VMEM((4, 4, BLOCK, rest // 2), BF16),
+            pltpu.VMEM((16, BLOCK, COLS // 2), F32),
             pltpu.VMEM((16, 16, 128), F32),
+            pltpu.VMEM((4, 8, 128), F32),
             pltpu.VMEM((4, 8, 128), F32),
             pltpu.VMEM((4, 8, 128), F32),
             pltpu.VMEM((16, 8, 128), F32),
             pltpu.VMEM((16, 8, 128), F32),
             pltpu.VMEM((16, 8, 128), F32),
+            pltpu.VMEM((4, 8, 128), F32),
+            pltpu.VMEM((4, 8, 128), F32),
             dma((5,)),
             dma((5,)),
             dma((5,)),
             dma((3, 8)),
             dma((3, 8)),
+            dma((3, 8)),
+            dma((3, 8)),
+            dma((3, 8)),
+            dma((3, 8)),
+            dma((2, 2)),
+            dma((4,)),
             dma((2, 2, 4)),
             dma((4, 4)),
             dma((3, 4)),
             dma((4, 4)),
             dma((4, 16)),
             dma((4, 16)),
+            dma((4, 4)),
         ],
         compiler_params=pltpu.CompilerParams(
             collective_id=0, has_side_effects=True, vmem_limit_bytes=58 * 2**20

time: 146 us -> 136 us (0.932)
  Pallas kernels: 144 us -> 135 us
    pallas_call x1, Pallas kernels: 144 us -> 135 us  [body(): pl.pallas_call(kernel, out_shape=jax.ShapeDtypeStruct((40, COLS), F32), i...]
where the time goes in v3:
time: 136 us
  Pallas kernels  135 us (99%)
  local copies, waits for them, and re-layouts  1.66 us (1%)
    pallas_call x1, Pallas kernels, body(): pl.pallas_call(kernel, out_shape=jax.ShapeDtypeStruct((40, COLS), F32), i...  135 us

profile of v3, /device:TPU:1, one launch (start us, length us, event | category | flops | bytes accessed | tf_op | source)
XLA Modules:
  0.0 136.2 jit_solution(2101363141446406622)
XLA Ops:
  0.0 134.5 %shard_map.28 = f32[40,1024]{1,0:T(8,128)} custom-call(bf16[512,5120]{1,0:T(8,128)(2,1)} %a_hbm.1, bf16[512,4,256]{2,1,0:T(4,128)(2,1)} %k_hbm.1), custom_call_target="tpu_custom_call" | custom-call | tf_op jit(solution)/shard_map/pallas_call | solution.py:774
  134.6 1.7 %reshape.3 = f32[40,4,256]{2,1,0:T(4,128)} reshape(f32[40,1024]{1,0:T(8,128)} %shard_map.28) | data formatting | bytes 327680 | tf_op jit(solution)/shard_map/reshape | solution.py:832

commit v4 on v3

--- a/solution.py
+++ b/solution.py
@@ -131,9 +131,9 @@
     a_hbm, k_hbm, o_ref,
     a_own, a_oth, k_raw, k_own, k_oth, grads, enc_x, recv_x, dec_x, enc_q, recv_q, recv_r, dec_q, sums_q,
     enc_y, recv_y, recv_z, enc_yq, recv_yq, dec_z,
-    rows_s, msg, msg_q, slots0, slots1, slots2, slots3, slots_q, slots_w,
+    rows_s, sums_z, msg, msg_q, slots0, slots1, slots2, slots3, slots_q, slots_w,
     load_sem, tok_send, tok_recv, x_send, x_recv, zq_send, zq_recv, xr_send, xr_recv,
-    yq_send, yq_recv, y_send, y_recv, z_send, z_recv, r_send, r_recv, q_sems,
+    yq_send, yq_recv, y_send, y_recv, z_send, z_recv, r_send, r_recv, q_sems, ready,
 ):
     me = lax.axis_index("dp")
     t = lax.axis_index("tensor")
@@ -146,22 +146,6 @@
     def plane16(k):
         return rank((y + k // 4) % 4, (z + k % 4) % 4, x, c), t
 
-    barrier = pltpu.get_barrier_semaphore()
-
-    def greet_group(k, _):
-        pl.semaphore_signal(barrier, inc=1, device_id=group16(k), device_id_type=MESH)
-        return _
-
-    def greet_plane(k, _):
-        pl.semaphore_signal(barrier, inc=1, device_id=plane16(k), device_id_type=MESH)
-        return _
-
-    def greet_other(k, _):
-        pl.semaphore_signal(
-            barrier, inc=1, device_id=(rank((y + k) % 4, z, x, 1 - c), t), device_id_type=MESH
-        )
-        return _
-
     def a_cols(core, i):
         return pl.ds(pl.multiple_of(core * HALF + i * TILE, 128), TILE)
 
@@ -176,11 +160,41 @@
         return _
 
     lax.fori_loop(0, 4, start_load, 0)
-    lax.fori_loop(1, 16, greet_group, 0)
-    lax.fori_loop(1, 16, greet_plane, 0)
-    lax.fori_loop(1, 4, greet_other, 0)
-    pl.semaphore_wait(barrier, 33)
+
+    barrier = pltpu.get_barrier_semaphore()
     other = (rank(y, z, x, 1 - c), t)
+
+    def greet_group(k, _):
+        pl.semaphore_signal(
+            barrier,
+            inc=1,
+            device_id=(rank(y, z, (x + k // 2) % 4, 0), (t + k % 2) % 2),
+            device_id_type=MESH,
+        )
+        return _
+
+    def greet_plane(k, _):
+        pl.semaphore_signal(
+            barrier,
+            inc=1,
+            device_id=(rank((y + k // 4) % 4, (z + k % 4) % 4, x, 0), t),
+            device_id_type=MESH,
+        )
+        return _
+
+    @pl.when(c == 0)
+    def open_pair():
+        pl.semaphore_signal(barrier, inc=1, device_id=other, device_id_type=MESH)
+
+    @pl.when(c == 1)
+    def answer_pair():
+        pl.semaphore_wait(barrier, 1)
+        pl.semaphore_signal(ready, inc=1, device_id=other, device_id_type=MESH)
+
+    @pl.when(c == 0)
+    def greet_chips():
+        pl.semaphore_wait(ready, 1)
+
     give_k = pltpu.make_async_remote_copy(
         k_own, k_oth, tok_send.at[4], tok_recv.at[4], device_id=other, device_id_type=MESH
     )
@@ -196,6 +210,12 @@
         )
 
     give_a(0).start()
+
+    @pl.when(c == 0)
+    def greet_all():
+        lax.fori_loop(1, 8, greet_group, 0)
+        lax.fori_loop(1, 16, greet_plane, 0)
+
     load_k.wait()
 
     def pack_k(n, _):
@@ -226,6 +246,12 @@
 
     zero = jnp.zeros((8, 128), F32)
     own_sq = lax.fori_loop(0, 4, own_tile, zero)
+
+    @pl.when(c == 0)
+    def all_greeted():
+        pl.semaphore_wait(barrier, 22)
+        pl.semaphore_signal(ready, inc=1, device_id=other, device_id_type=MESH)
+
     give_k.wait_recv()
 
     def other_tile(i, sums):
@@ -238,6 +264,11 @@
         return cross + fold(own * tile), oth_sq + fold(tile * tile)
 
     cross, oth_sq = lax.fori_loop(0, 4, other_tile, (zero, zero))
+
+    @pl.when(c == 1)
+    def told():
+        pl.semaphore_wait(ready, 1)
+
     own_sq, oth_sq, cross = total(own_sq), total(oth_sq), total(cross)
     lower_sq = jnp.where(c == 0, own_sq, oth_sq)
     upper_sq = jnp.where(c == 0, oth_sq, own_sq)
@@ -644,9 +675,36 @@
 
     lax.fori_loop(0, 4, yq_arrival, 0)
 
-    def z_arrival(n, _):
-        source = (z + 1 + n // 4) % 4
-        sy = n % 4
+    def group_pairs(a, b):
+        return [(i, j) for i in range(4) for j in range(4) if a != b or i <= j]
+
+    def products(a, b, first, last, sums):
+        def one(n, sums):
+            r = pl.ds(pl.multiple_of(n * 8, 8), 8)
+            sums = list(sums)
+            for l in range(first, last, 128):
+                v = [dec_z[i * 4 + (z + 4 - a) % 4, r, l : l + 128] for i in range(4)]
+                w = v if a == b else [dec_z[i * 4 + (z + 4 - b) % 4, r, l : l + 128] for i in range(4)]
+                for m, (i, j) in enumerate(group_pairs(a, b)):
+                    sums[m] = sums[m] + v[i] * w[j]
+            return tuple(sums)
+
+        return lax.fori_loop(0, 10, one, tuple(sums))
+
+    def finish_rows(a, b, sums):
+        for (i, j), total_ij in zip(group_pairs(a, b), sums):
+            line = jnp.sum(total_ij, axis=0, keepdims=True)
+            first, second = i * 4 + (z + 4 - a) % 4, j * 4 + (z + 4 - b) % 4
+            rows_s[first, pl.ds(second, 1), :] = line
+            rows_s[second, pl.ds(first, 1), :] = line
+
+    blocks = [(a, b) for a in range(4) for b in range(a + 1)]
+    for n, (a, b) in enumerate(blocks):
+        sums = products(a, b, PART // 2, COLS // 2, [zero] * len(group_pairs(a, b)))
+        for m, value in enumerate(sums):
+            sums_z[n, m] = value
+
+    def z_arrival(source, sy):
         pltpu.make_async_copy(
             recv_z.at[source, sy], recv_z.at[source, sy], z_recv.at[source, sy]
         ).wait()
@@ -654,29 +712,19 @@
             dec_z[sy * 4 + source, r : r + 16, 0 : PART // 2] = decode(
                 recv_z[source, sy, r : r + 16, :]
             )
-        return _
-
-    lax.fori_loop(0, 12, z_arrival, 0)
-
-    for bi in range(0, 16, 4):
-        for bj in range(bi, 16, 4):
-            pairs = [(i, j) for i in range(bi, bi + 4) for j in range(bj, bj + 4) if i <= j]
-
-            def products(n, sums):
-                r = pl.ds(pl.multiple_of(n * 8, 8), 8)
-                sums = list(sums)
-                for l in range(0, 512, 128):
-                    v = {i: dec_z[i, r, l : l + 128] for i in {i for p in pairs for i in p}}
-                    for m, (i, j) in enumerate(pairs):
-                        sums[m] = sums[m] + v[i] * v[j]
-                return tuple(sums)
-
-            sums = lax.fori_loop(0, 10, products, (zero,) * len(pairs))
-            for (i, j), s in zip(pairs, sums):
-                line = jnp.sum(s, axis=0, keepdims=True)
-                rows_s[i, j : j + 1, :] = line
-                if i != j:
-                    rows_s[j, i : i + 1, :] = line
+
+    for a in range(4):
+        if a:
+
+            def arrive_z(sy, _):
+                z_arrival((z + 4 - a) % 4, sy)
+                return _
+
+            lax.fori_loop(0, 4, arrive_z, 0)
+        for b in range(a + 1):
+            n = blocks.index((a, b))
+            before = [sums_z[n, m] for m in range(len(group_pairs(a, b)))]
+            finish_rows(a, b, products(a, b, 0, PART // 2, before))
     row16, lane16 = iotas(16)
     gram = jnp.zeros((16, 128), F32)
     for i in range(16):
@@ -798,6 +846,7 @@
             pltpu.VMEM((4, 4, BLOCK, rest // 2), BF16),
             pltpu.VMEM((16, BLOCK, COLS // 2), F32),
             pltpu.VMEM((16, 16, 128), F32),
+            pltpu.VMEM((10, 16, 8, 128), F32),
             pltpu.VMEM((4, 8, 128), F32),
             pltpu.VMEM((4, 8, 128), F32),
             pltpu.VMEM((4, 8, 128), F32),
@@ -824,6 +873,7 @@
             dma((4, 16)),
             dma((4, 16)),
             dma((4, 4)),
+            pltpu.SemaphoreType.REGULAR,
         ],
         compiler_params=pltpu.CompilerParams(
             collective_id=0, has_side_effects=True, vmem_limit_bytes=58 * 2**20

time: 136 us -> 132 us (0.971)
  Pallas kernels: 135 us -> 130 us
    pallas_call x1, Pallas kernels: 135 us -> 130 us  [body(): pl.pallas_call(kernel, out_shape=jax.ShapeDtypeStruct((40, COLS), F32), i...]
where the time goes in v4:
time: 132 us
  Pallas kernels  130 us (98%)
  local copies, waits for them, and re-layouts  1.66 us (1%)
    pallas_call x1, Pallas kernels, body(): pl.pallas_call(kernel, out_shape=jax.ShapeDtypeStruct((40, COLS), F32), i...  130 us

profile of v4, /device:TPU:1, one launch (start us, length us, event | category | flops | bytes accessed | tf_op | source)
XLA Modules:
  0.0 132.1 jit_solution(4753280599706037140)
XLA Ops:
  0.0 130.4 %shard_map.28 = f32[40,1024]{1,0:T(8,128)} custom-call(bf16[512,5120]{1,0:T(8,128)(2,1)} %a_hbm.1, bf16[512,4,256]{2,1,0:T(4,128)(2,1)} %k_hbm.1), custom_call_target="tpu_custom_call" | custom-call | tf_op jit(solution)/shard_map/pallas_call | solution.py:822
  130.4 1.7 %reshape.3 = f32[40,4,256]{2,1,0:T(4,128)} reshape(f32[40,1024]{1,0:T(8,128)} %shard_map.28) | data formatting | bytes 327680 | tf_op jit(solution)/shard_map/reshape | solution.py:882

commit v5 on v4

--- a/solution.py
+++ b/solution.py
@@ -129,16 +129,16 @@
 
 def kernel(
     a_hbm, k_hbm, o_ref,
-    a_own, a_oth, k_raw, k_own, k_oth, grads, enc_x, recv_x, dec_x, enc_q, recv_q, recv_r, dec_q, sums_q,
+    a_own, a_oth, k_raw, k_own, k_oth, grads, recv_g, msg_g, slots_g, enc_x, recv_x, dec_x, enc_q, recv_q, recv_r, dec_q, sums_q,
     enc_y, recv_y, recv_z, enc_yq, recv_yq, dec_z,
-    rows_s, sums_z, msg, msg_q, slots0, slots1, slots2, slots3, slots_q, slots_w,
+    rows_s, sums_z, msg0, msg1, msg2, msg3, msg_q, slots0, slots1, slots2, slots3, slots_q, slots_w,
     load_sem, tok_send, tok_recv, x_send, x_recv, zq_send, zq_recv, xr_send, xr_recv,
-    yq_send, yq_recv, y_send, y_recv, z_send, z_recv, r_send, r_recv, q_sems, ready,
+    yq_send, yq_recv, y_send, y_recv, z_send, z_recv, r_send, r_recv, q_sems, g_sems, ready,
 ):
     me = lax.axis_index("dp")
     t = lax.axis_index("tensor")
     y, z, x, c = coords(me)
-    row8, lane8 = iotas(8)
+    lane1 = lax.broadcasted_iota(jnp.int32, (1, 128), 1)
 
     def group16(k):
         return rank(y, z, (x + k // 4) % 4, (c + (k // 2) % 2) % 2), (t + k % 2) % 2
@@ -252,6 +252,25 @@
         pl.semaphore_wait(barrier, 22)
         pl.semaphore_signal(ready, inc=1, device_id=other, device_id_type=MESH)
 
+    @pl.when(c == 1)
+    def told():
+        pl.semaphore_wait(ready, 1)
+
+    def along_x(d):
+        return rank(y, z, (x + d) % 4, c), t
+
+    def raw_copy(which, d):
+        return pltpu.make_async_remote_copy(
+            grads.at[which, (x + d) % 4, :, pl.ds(0, PART)],
+            recv_g.at[which, d - 1],
+            g_sems.at[0, which * 3 + d - 1],
+            g_sems.at[1, which * 3 + d - 1],
+            device_id=along_x(d),
+            device_id_type=MESH,
+        )
+
+    for d in (2, 1, 3):
+        raw_copy(0, d).start()
     give_k.wait_recv()
 
     def other_tile(i, sums):
@@ -263,23 +282,25 @@
         own = grads[0, pl.ds(i * 8, 8)].astype(F32).reshape(TILE, COLS)
         return cross + fold(own * tile), oth_sq + fold(tile * tile)
 
-    cross, oth_sq = lax.fori_loop(0, 4, other_tile, (zero, zero))
-
-    @pl.when(c == 1)
-    def told():
-        pl.semaphore_wait(ready, 1)
+    sums = other_tile(0, (zero, zero))
+    for d in (2, 1, 3):
+        raw_copy(1, d).start()
+    cross, oth_sq = lax.fori_loop(1, 4, other_tile, sums)
 
     own_sq, oth_sq, cross = total(own_sq), total(oth_sq), total(cross)
     lower_sq = jnp.where(c == 0, own_sq, oth_sq)
     upper_sq = jnp.where(c == 0, oth_sq, own_sq)
 
-    def entry(i, j):
-        return (row8 == i) & (lane8 == j)
-
-    def exchange(stage, slots, first, last, target):
+    def spot(lane, value):
+        return jnp.where(lane1 == lane, value, 0.0)
+
+    def pick(table, lane):
+        return total(jnp.where(lane1 == lane, table, 0.0))
+
+    def exchange(stage, msg, slots, first, last, target):
         def go(k, _):
             pltpu.make_async_remote_copy(
-                msg.at[stage],
+                msg,
                 slots.at[k],
                 r_send.at[stage, k],
                 r_recv.at[stage, k],
@@ -293,7 +314,7 @@
             return table + slots[k]
 
         lax.fori_loop(first, last, go, 0)
-        return lax.fori_loop(first, last, arrive, msg[stage])
+        return lax.fori_loop(first, last, arrive, msg[...])
 
     def finish_exchange(stage, slots, first, last):
         def done(k, _):
@@ -302,31 +323,35 @@
 
         lax.fori_loop(first, last, done, 0)
 
-    msg[0] = (
-        jnp.where(entry(0, 0), lower_sq, 0.0)
-        + jnp.where(entry(1, 1), upper_sq, 0.0)
-        + jnp.where(entry(0, 1) | entry(1, 0), cross, 0.0)
-    )
-    gram = exchange(0, slots0, 1, 4, group16)
-
-    def pick(table, i, j):
-        return total(jnp.where(entry(i, j), table, 0.0))
-
-    lower_sq, upper_sq, cross = pick(gram, 0, 0), pick(gram, 1, 1), pick(gram, 0, 1)
+    msg0[...] = spot(0, lower_sq) + spot(1, upper_sq) + spot(2, cross)
+    table = exchange(0, msg0, slots0, 1, 4, group16)
+    lower_sq, upper_sq, cross = pick(table, 0), pick(table, 1), pick(table, 2)
     w_low, w_up = pair_weights(lower_sq, upper_sq, cross)
     bound = 2.0 * (w_low * w_low * lower_sq + w_up * w_up * upper_sq) + 1e-36
     scale = TOP * lax.rsqrt(bound)
     inverse1 = 1.0 / scale
-    w_own = wide(scale * jnp.where(c == 0, w_low, w_up))
-    w_oth = wide(scale * jnp.where(c == 0, w_up, w_low))
+    w_own = scale * jnp.where(c == 0, w_low, w_up)
+    w_oth = scale * jnp.where(c == 0, w_up, w_low)
+    msg_g[...] = spot(0, w_own) + spot(1, w_oth)
+
+    def pair_copy(d):
+        return pltpu.make_async_remote_copy(
+            msg_g,
+            slots_g.at[d],
+            g_sems.at[0, 5 + d],
+            g_sems.at[1, 5 + d],
+            device_id=along_x(d),
+            device_id_type=MESH,
+        )
+
+    for d in (2, 1, 3):
+        pair_copy(d).start()
+    w_own, w_oth = wide(w_own), wide(w_oth)
 
     def pair_of(block, r, l):
         own = grads[0, block, r : r + 16, l : l + 128].astype(F32)
         oth = grads[1, block, r : r + 16, l : l + 128].astype(F32)
         return w_own * own + w_oth * oth
-
-    def along_x(d):
-        return rank(y, z, (x + d) % 4, c), t
 
     def along_z(d):
         return rank(y, (z + d) % 4, x, c), t
@@ -383,22 +408,22 @@
                 zq_copy(dz, yy, dx).start()
 
     def send_far(m, _):
-        x_send_block(m)
+        x_send_block(1 + m)
         q_send_block(m, 2)
         return _
 
     def send_near(k, _):
-        x_send_block(2 + k)
+        x_send_block(3 + k)
         q_send_block(k // 2, 1 + 2 * (k % 2))
         return _
 
     def send_own(m, _):
-        x_send_block(6 + m)
         q_send_block(m, 0)
         return _
 
     lax.fori_loop(0, 2, send_far, 0)
     lax.fori_loop(0, 4, send_near, 0)
+    x_send_block(7)
     lax.fori_loop(0, 2, send_own, 0)
 
     def x_own_block(b, _):
@@ -409,6 +434,30 @@
 
     lax.fori_loop(0, 8, x_own_block, 0)
     pairs4 = [(i, j) for i in range(4) for j in range(i, 4)]
+
+    def x_products(b, sums):
+        sums = list(sums)
+        for r in range(0, BLOCK, 8):
+            for l in range(0, PART, 128):
+                v = [dec_x[i, b, r : r + 8, l : l + 128] for i in range(4)]
+                for n, (i, j) in enumerate(pairs4):
+                    sums[n] = sums[n] + v[i] * v[j]
+        return tuple(sums)
+
+    def x_recv_raw(sums):
+        for d in (1, 3, 2):
+            raw_copy(0, d).wait_recv()
+            raw_copy(1, d).wait_recv()
+            pair_copy(d).wait_recv()
+            w_first, w_second = wide(pick(slots_g[d], 0)), wide(pick(slots_g[d], 1))
+            for r in range(0, BLOCK, 16):
+                for l in range(0, PART, 128):
+                    first = recv_g[0, d - 1, r : r + 16, l : l + 128].astype(F32)
+                    second = recv_g[1, d - 1, r : r + 16, l : l + 128].astype(F32)
+                    dec_x[(x + 4 - d) % 4, 0, r : r + 16, l : l + 128] = (
+                        w_first * first + w_second * second
+                    )
+        return x_products(0, sums)
 
     def x_recv_block(b, sums):
         for d in (1, 3, 2):
@@ -419,13 +468,7 @@
                     dec_x[source, b, r : r + 16, l : l + 256] = decode(
                         recv_x[d - 1, b, r : r + 16, l : l + 256]
                     )
-        sums = list(sums)
-        for r in range(0, BLOCK, 8):
-            for l in range(0, PART, 128):
-                v = [dec_x[i, b, r : r + 8, l : l + 128] for i in range(4)]
-                for n, (i, j) in enumerate(pairs4):
-                    sums[n] = sums[n] + v[i] * v[j]
-        return tuple(sums)
+        return x_products(b, sums)
 
     def relay(yy, dx):
         for dz in (0, 1, 3, 2):
@@ -441,7 +484,7 @@
         relay(k // 2, 1 + 2 * (k % 2))
         return _
 
-    sums = lax.fori_loop(0, 4, x_recv_block, (zero,) * 10)
+    sums = lax.fori_loop(1, 4, x_recv_block, x_recv_raw((zero,) * 10))
     lax.fori_loop(0, 2, relay_far, 0)
     sums = lax.fori_loop(4, 8, x_recv_block, sums)
     lax.fori_loop(0, 4, relay_near, 0)
@@ -503,23 +546,22 @@
         )
 
     def tile_of(sums):
-        table = jnp.zeros((8, 128), F32)
-        for (i, j), s in zip(pairs4, sums):
-            table = table + jnp.where(entry(i, j), total(s), 0.0)
-        return table
+        return sum((spot(n, total(s)) for n, s in enumerate(sums[1:], 1)), spot(0, total(sums[0])))
 
     for dz in (2, 1, 3):
         msg_q[dz] = tile_of([sums_q[dz, n] for n in range(10)])
         q_copy(dz).start()
-    table = jnp.where(entry(4, x), 0.25 * inverse1, 0.0)
+    table = spot(16 + x, 0.25 * inverse1)
     table = table + tile_of([s + sums_q[0, n] for n, s in enumerate(sums)])
     for dz in (1, 3, 2):
         q_copy(dz).wait_recv()
         table = table + slots_q[dz]
-    msg[1] = table
-    table = exchange(1, slots1, 1, 16, group16)
-    inv = [pick(table, 4, i) for i in range(4)]
-    weight, bound = solve4({(i, j): pick(table, i, j) * inv[i] * inv[j] for i, j in pairs4})
+    msg1[...] = table
+    table = exchange(1, msg1, slots1, 1, 16, group16)
+    inv = [pick(table, 16 + i) for i in range(4)]
+    weight, bound = solve4(
+        {(i, j): pick(table, n) * inv[i] * inv[j] for n, (i, j) in enumerate(pairs4)}
+    )
     scale = TOP * lax.rsqrt(bound)
     inverse3 = 1.0 / scale
     w_own_z = [weight[i] * inv[i] * scale for i in range(4)]
@@ -534,10 +576,9 @@
             device_id_type=MESH,
         )
 
-    table = jnp.zeros((8, 128), F32)
-    for i in range(4):
-        table = table + jnp.where(entry(0, i), w_own_z[i], 0.0)
-    msg_q[0] = table
+    msg_q[0] = (spot(0, w_own_z[0]) + spot(1, w_own_z[1])) + (
+        spot(2, w_own_z[2]) + spot(3, w_own_z[3])
+    )
     for dz in (2, 1, 3):
         w_copy(dz).start()
     w_x = [wide(w_own_z[i], 40) for i in range(4)]
@@ -628,7 +669,7 @@
     for dz in range(4):
         if dz:
             w_copy(dz).wait_recv()
-            w_by_z.append([wide(pick(slots_w[dz], 0, i), 40) for i in range(4)])
+            w_by_z.append([wide(pick(slots_w[dz], i), 40) for i in range(4)])
         else:
             w_by_z.append(w_x)
 
@@ -689,7 +730,7 @@
                     sums[m] = sums[m] + v[i] * w[j]
             return tuple(sums)
 
-        return lax.fori_loop(0, 10, one, tuple(sums))
+        return lax.fori_loop(0, 10, one, tuple(sums), unroll=5)
 
     def finish_rows(a, b, sums):
         for (i, j), total_ij in zip(group_pairs(a, b), sums):
@@ -729,13 +770,29 @@
     gram = jnp.zeros((16, 128), F32)
     for i in range(16):
         gram = gram + jnp.where(lane16 == i, jnp.sum(rows_s[i], axis=1, keepdims=True), 0.0)
-    msg[2] = gram[0:8] + pltpu.roll(gram[8:16], 64, 1)
-    partial = exchange(2, slots2, 1, 16, group16)
-    msg[3] = partial + jnp.where(entry(0, 32 + 4 * y + z), inverse3, 0.0)
-    table = exchange(3, slots3, 1, 16, plane16)
-    inv_row = jnp.where(lane8[0:1] < 16, pltpu.roll(table, 96, 1)[0:1], 0.0)
+
+    def flat(part):
+        line = jnp.where(row16[0:8] == 0, part, 0.0)
+        for i in range(1, 8):
+            line = line + jnp.where(row16[0:8] == i, pltpu.roll(part, 16 * i, 1), 0.0)
+        return jnp.sum(line, axis=0, keepdims=True)
+
+    def square(line):
+        full = wide(line, 8)
+        part = jnp.where(row16[0:8] == 0, full, 0.0)
+        for i in range(1, 8):
+            part = part + jnp.where(row16[0:8] == i, pltpu.roll(full, 128 - 16 * i, 1), 0.0)
+        return part
+
+    msg2[0:1] = flat(gram[0:8])
+    msg2[1:2] = flat(gram[8:16])
+    partial = exchange(2, msg2, slots2, 1, 16, group16)
+    msg3[0:2] = partial
+    msg3[2:4] = wide(spot(4 * y + z, inverse3), 2)
+    table = exchange(3, msg3, slots3, 1, 16, plane16)
+    inv_row = table[2:3]
     inv_col = jnp.sum(jnp.where(row16 == lane16, inv_row, 0.0), axis=1, keepdims=True)
-    gram = jnp.concatenate([table, pltpu.roll(table, 64, 1)], axis=0)
+    gram = jnp.concatenate([square(table[0:1]), square(table[1:2])], axis=0)
     gram = jnp.where(lane16 < 16, gram, 0.0) * inv_row * inv_col
     weight = solve(gram, 16) * inv_col
     w_z = [wide(weight[i : i + 1], 8) for i in range(16)]
@@ -763,7 +820,11 @@
             x_copy(d, b).wait_send()
         return _
 
-    lax.fori_loop(0, 8, x_done, 0)
+    lax.fori_loop(1, 8, x_done, 0)
+    for d in (1, 2, 3):
+        raw_copy(0, d).wait_send()
+        raw_copy(1, d).wait_send()
+        pair_copy(d).wait_send()
 
     def zq_done(n, _):
         for dz in (1, 2, 3):
@@ -831,6 +892,9 @@
             pltpu.VMEM((tokens, COLS), BF16),
             pltpu.VMEM((tokens, COLS), BF16),
             pltpu.VMEM((2, 32, BLOCK, COLS), BF16),
+            pltpu.VMEM((2, 3, BLOCK, PART), BF16),
+            pltpu.VMEM((1, 128), F32),
+            pltpu.VMEM((4, 1, 128), F32),
             pltpu.VMEM((3, 8, BLOCK, PART), BF16),
             pltpu.VMEM((3, 8, BLOCK, PART), BF16),
             pltpu.VMEM((4, 8, BLOCK, PART), F32),
@@ -847,14 +911,17 @@
             pltpu.VMEM((16, BLOCK, COLS // 2), F32),
             pltpu.VMEM((16, 16, 128), F32),
             pltpu.VMEM((10, 16, 8, 128), F32),
-            pltpu.VMEM((4, 8, 128), F32),
-            pltpu.VMEM((4, 8, 128), F32),
-            pltpu.VMEM((4, 8, 128), F32),
-            pltpu.VMEM((16, 8, 128), F32),
-            pltpu.VMEM((16, 8, 128), F32),
-            pltpu.VMEM((16, 8, 128), F32),
-            pltpu.VMEM((4, 8, 128), F32),
-            pltpu.VMEM((4, 8, 128), F32),
+            pltpu.VMEM((1, 128), F32),
+            pltpu.VMEM((1, 128), F32),
+            pltpu.VMEM((2, 128), F32),
+            pltpu.VMEM((4, 128), F32),
+            pltpu.VMEM((4, 1, 128), F32),
+            pltpu.VMEM((4, 1, 128), F32),
+            pltpu.VMEM((16, 1, 128), F32),
+            pltpu.VMEM((16, 2, 128), F32),
+            pltpu.VMEM((16, 4, 128), F32),
+            pltpu.VMEM((4, 1, 128), F32),
+            pltpu.VMEM((4, 1, 128), F32),
             dma((5,)),
             dma((5,)),
             dma((5,)),
@@ -873,6 +940,7 @@
             dma((4, 16)),
             dma((4, 16)),
             dma((4, 4)),
+            dma((2, 9)),
             pltpu.SemaphoreType.REGULAR,
         ],
         compiler_params=pltpu.CompilerParams(

time: 132 us -> 128 us (0.970)
  Pallas kernels: 130 us -> 126 us
    pallas_call x1, Pallas kernels: 130 us -> 126 us  [body(): pl.pallas_call(kernel, out_shape=jax.ShapeDtypeStruct((40, COLS), F32), i...]
where the time goes in v5:
time: 128 us
  Pallas kernels  126 us (98%)
  local copies, waits for them, and re-layouts  1.66 us (1%)
    pallas_call x1, Pallas kernels, body(): pl.pallas_call(kernel, out_shape=jax.ShapeDtypeStruct((40, COLS), F32), i...  126 us

profile of v5, /device:TPU:1, one launch (start us, length us, event | category | flops | bytes accessed | tf_op | source)
XLA Modules:
  0.0 128.0 jit_solution(16498945967061006352)
XLA Ops:
  0.0 126.3 %shard_map.28 = f32[40,1024]{1,0:T(8,128)} custom-call(bf16[512,5120]{1,0:T(8,128)(2,1)} %a_hbm.1, bf16[512,4,256]{2,1,0:T(4,128)(2,1)} %k_hbm.1), custom_call_target="tpu_custom_call" | custom-call | tf_op jit(solution)/shard_map/pallas_call | solution.py:883
  126.3 1.7 %reshape.3 = f32[40,4,256]{2,1,0:T(4,128)} reshape(f32[40,1024]{1,0:T(8,128)} %shard_map.28) | data formatting | bytes 327680 | tf_op jit(solution)/shard_map/reshape | solution.py:950

commit v6 on v5

--- a/solution.py
+++ b/solution.py
@@ -408,13 +408,13 @@
                 zq_copy(dz, yy, dx).start()
 
     def send_far(m, _):
+        q_send_block(m, 2)
         x_send_block(1 + m)
-        q_send_block(m, 2)
         return _
 
     def send_near(k, _):
+        q_send_block(k // 2, 1 + 2 * (k % 2))
         x_send_block(3 + k)
-        q_send_block(k // 2, 1 + 2 * (k % 2))
         return _
 
     def send_own(m, _):
@@ -647,8 +647,8 @@
         pltpu.make_async_copy(recv_y.at[sy, zt], recv_y.at[sy, zt], y_recv.at[sy, zt]).wait()
 
     def z_relay(n, _):
-        d = 1 + n // 4
-        sy = n % 4
+        d = 1 + n % 3
+        sy = (y + n // 3) % 4
         y_arrival(sy, (z + d) % 4)
         z_copy(d, sy).start()
         return _

time: 128 us -> 128 us (level)
  no operation moved by 1% of the time
where the time goes in v6:
time: 128 us
  Pallas kernels  126 us (98%)
  local copies, waits for them, and re-layouts  1.66 us (1%)
    pallas_call x1, Pallas kernels, body(): pl.pallas_call(kernel, out_shape=jax.ShapeDtypeStruct((40, COLS), F32), i...  126 us

profile of v6, /device:TPU:1, one launch (start us, length us, event | category | flops | bytes accessed | tf_op | source)
XLA Modules:
  0.0 128.1 jit_solution(2967575300888183623)
XLA Ops:
  0.0 126.4 %shard_map.28 = f32[40,1024]{1,0:T(8,128)} custom-call(bf16[512,5120]{1,0:T(8,128)(2,1)} %a_hbm.1, bf16[512,4,256]{2,1,0:T(4,128)(2,1)} %k_hbm.1), custom_call_target="tpu_custom_call" | custom-call | tf_op jit(solution)/shard_map/pallas_call | solution.py:883
  126.4 1.7 %reshape.3 = f32[40,4,256]{2,1,0:T(4,128)} reshape(f32[40,1024]{1,0:T(8,128)} %shard_map.28) | data formatting | bytes 327680 | tf_op jit(solution)/shard_map/reshape | solution.py:950

commit v7 on v5

--- a/solution.py
+++ b/solution.py
@@ -510,7 +510,7 @@
             zq_copy(dz, yy, 0).wait_recv()
         q_decode(0, yy)
 
-    def q_gram(yy):
+    def q_gram(yy, first, last):
         def one(dz, _):
             sums = [zero if yy == 0 else sums_q[dz, n] for n in range(10)]
             for r in range(0, BLOCK, 8):
@@ -522,18 +522,18 @@
                 sums_q[dz, n] = sums[n]
             return _
 
-        lax.fori_loop(0, 4, one, 0)
+        lax.fori_loop(first, last, one, 0)
 
     q_decode(2, 0)
     q_decode(2, 1)
     q_decode(1, 0)
     q_decode(3, 0)
     q_own(0)
-    q_gram(0)
+    q_gram(0, 0, 4)
     q_decode(1, 1)
     q_decode(3, 1)
     q_own(1)
-    q_gram(1)
+    q_gram(1, 1, 4)
 
     def q_copy(dz):
         return pltpu.make_async_remote_copy(
@@ -551,6 +551,7 @@
     for dz in (2, 1, 3):
         msg_q[dz] = tile_of([sums_q[dz, n] for n in range(10)])
         q_copy(dz).start()
+    q_gram(1, 0, 1)
     table = spot(16 + x, 0.25 * inverse1)
     table = table + tile_of([s + sums_q[0, n] for n, s in enumerate(sums)])
     for dz in (1, 3, 2):

time: 128 us -> 128 us (level)
  no operation moved by 1% of the time
where the time goes in v7:
time: 128 us
  Pallas kernels  126 us (98%)
  local copies, waits for them, and re-layouts  1.66 us (1%)
    pallas_call x1, Pallas kernels, body(): pl.pallas_call(kernel, out_shape=jax.ShapeDtypeStruct((40, COLS), F32), i...  126 us

profile of v7, /device:TPU:1, one launch (start us, length us, event | category | flops | bytes accessed | tf_op | source)
XLA Modules:
  0.0 127.9 jit_solution(10248223932218434300)
XLA Ops:
  0.0 126.2 %shard_map.28 = f32[40,1024]{1,0:T(8,128)} custom-call(bf16[512,5120]{1,0:T(8,128)(2,1)} %a_hbm.1, bf16[512,4,256]{2,1,0:T(4,128)(2,1)} %k_hbm.1), custom_call_target="tpu_custom_call" | custom-call | tf_op jit(solution)/shard_map/pallas_call | solution.py:884
  126.2 1.7 %reshape.3 = f32[40,4,256]{2,1,0:T(4,128)} reshape(f32[40,1024]{1,0:T(8,128)} %shard_map.28) | data formatting | bytes 327680 | tf_op jit(solution)/shard_map/reshape | solution.py:951
